TPU v7x, 32 devices: a whole 2x2x4 slice. The times are simulated.
32 devices in a mesh: section: 2 (over core), expert: 4 (over z), tp: 4 (over y, x).
Axes of the slice: x: 2, y: 2, z: 4, core: 2. Of those that a mesh axis runs over, the one named last changes fastest.
Arguments:
- tokens: bfloat16 [512, 4096], P('expert', ('tp', 'section')), may hold values from -6 to 6
- out_grad: bfloat16 [512, 4096], P('expert', ('tp', 'section')), may hold values from -12 to 12
- expert_ids: int32 [512, 2], P('expert'), may hold values from 0 to 3, all different within a row; in each aligned block of 128 rows (0 to 127, 128 to 255, ...) at most 72 rows name the same one
- combine: float32 [512, 2], P('expert'), may hold values from 0.05 to 0.5
- w_gate: bfloat16 [4, 4096, 768], P('expert', 'tp', 'section'), may hold values from -0.09375 to 0.09375
- w_up: bfloat16 [4, 4096, 768], P('expert', 'tp', 'section'), may hold values from -0.09375 to 0.09375
- w_down: bfloat16 [4, 768, 4096], P('expert', 'section', 'tp'), may hold values from -0.21875 to 0.21875
Outputs:
- token_grad: bfloat16 [512, 4096], P('expert', ('tp', 'section'))
- gate_weight_grad: bfloat16 [4, 4096, 768], P('expert', 'tp', 'section')
- up_weight_grad: bfloat16 [4, 4096, 768], P('expert', 'tp', 'section')
- down_weight_grad: bfloat16 [4, 768, 4096], P('expert', 'section', 'tp')
Inputs may be any that keep to these rules, and one draw needn't show every extreme that they name: `expert_ids`: each row names 2 different experts; among the 128 rows of one index of expert no expert is named more than 72 times, a bound that some block reaches.
All inputs are finite; a program needn't handle non-finite values.
Results may differ from a plain program's by a relative error of at most 0.025.
Values may be sent and summed in bfloat16 or wider, within the bound.
A program may use at most 64 MiB of HBM per device.

v0:
```python
import jax
import jax.numpy as jnp
from jax import lax
from jax.sharding import PartitionSpec as P


def block_slots(expert_ids, experts, capacity):
    flat_ids = expert_ids.reshape(-1)
    pick_count = flat_ids.shape[0]
    onehot = (flat_ids[:, None] == jnp.arange(experts, dtype=jnp.int32)[None, :]).astype(jnp.int32)
    earlier = jnp.cumsum(onehot, axis=0) - onehot
    slot_index = jnp.sum(earlier * onehot, axis=1)
    place_index = flat_ids * capacity + slot_index
    source = (
        jnp.zeros((experts * capacity,), jnp.int32)
        .at[place_index]
        .set(jnp.arange(pick_count, dtype=jnp.int32))
    )
    filled = (
        jnp.zeros((experts * capacity,), jnp.int32)
        .at[place_index]
        .set(jnp.ones((pick_count,), jnp.int32))
    )
    return (slot_index, source.reshape(experts, capacity), filled.reshape(experts, capacity))


def round_back(values):
    return lax.optimization_barrier(values.astype(jnp.bfloat16)).astype(jnp.float32)


def local_grads(gate_pre, up_pre, hidden_grad):
    sigmoid_g = jax.nn.sigmoid(gate_pre)
    activated = (gate_pre * sigmoid_g * up_pre).astype(jnp.bfloat16)
    gate_grad = (hidden_grad * up_pre * sigmoid_g * (1.0 + gate_pre * (1.0 - sigmoid_g))).astype(
        jnp.bfloat16
    )
    up_grad = (hidden_grad * gate_pre * sigmoid_g).astype(jnp.bfloat16)
    return (activated, gate_grad, up_grad)


def fill_buffers(source, filled, combine, top_count, features, grad_rows):
    tok_count = features.shape[0]
    token_index = source // top_count
    keep_mask = (filled > 0)[:, :, None]
    positions = jnp.arange(tok_count, dtype=jnp.int32)[None, None, :]
    selector = jnp.logical_and(token_index[:, :, None] == positions, keep_mask).astype(jnp.bfloat16)
    rows_in = jnp.einsum(
        "ect,td->ecd", selector, features, preferred_element_type=jnp.float32
    ).astype(jnp.bfloat16)
    picked_grad = jnp.einsum("ect,td->ecd", selector, grad_rows, preferred_element_type=jnp.float32)
    weight = combine.reshape(-1)[source]
    grad_in = (picked_grad * weight[:, :, None]).astype(jnp.bfloat16)
    return (rows_in, grad_in)


def token_picker(pick_rows, tok_dev, top_count, row_count):
    columns = jnp.arange(row_count, dtype=jnp.int32)[None, None, :]
    hits = (pick_rows.reshape(tok_dev, top_count)[:, :, None] == columns).astype(jnp.int32)
    return jnp.sum(hits, axis=1)


def contract_rows(left_side, right_side):
    return lax.dot_general(
        left_side, right_side, (((0,), (0,)), ((), ())), preferred_element_type=jnp.float32
    )


def contract_last(left_side, right_side):
    return lax.dot_general(
        left_side, right_side, (((1,), (1,)), ((), ())), preferred_element_type=jnp.float32
    )


def on_device(tokens, out_grad, expert_ids, combine, w_gate, w_up, w_down):
    tok_dev, top_count = expert_ids.shape
    experts = lax.axis_size("expert")
    capacity = (tok_dev * top_count * 9 + 8 * experts - 1) // (8 * experts)
    slot_index, source, filled = block_slots(expert_ids, experts, capacity)
    features, grad_rows = (
        lax.all_gather(tokens, "section", axis=1, tiled=True),
        lax.all_gather(out_grad, "section", axis=1, tiled=True),
    )
    send_rows, send_grads = fill_buffers(source, filled, combine, top_count, features, grad_rows)
    got_rows, got_grads = (
        lax.all_to_all(send_rows, "expert", split_axis=0, concat_axis=0, tiled=True),
        lax.all_to_all(send_grads, "expert", split_axis=0, concat_axis=0, tiled=True),
    )
    width_dev = got_rows.shape[2]
    rows_in = got_rows.reshape(-1, width_dev)
    grad_in = got_grads.reshape(-1, width_dev)
    gate_w = w_gate[0]
    up_w = w_up[0]
    down_w = w_down[0]
    gate_part = round_back(jnp.dot(rows_in, gate_w, preferred_element_type=jnp.float32))
    up_part = round_back(jnp.dot(rows_in, up_w, preferred_element_type=jnp.float32))
    hidden_part = round_back(contract_last(grad_in, down_w))
    gate_pre, up_pre, hidden_grad = (
        lax.psum(gate_part.astype(jnp.bfloat16), "tp").astype(jnp.float32),
        lax.psum(up_part.astype(jnp.bfloat16), "tp").astype(jnp.float32),
        lax.psum(hidden_part.astype(jnp.bfloat16), "tp").astype(jnp.float32),
    )
    activated, gate_grad, up_grad = local_grads(gate_pre, up_pre, hidden_grad)
    row_float = contract_last(gate_grad, gate_w) + contract_last(up_grad, up_w)
    flat_ids = expert_ids.reshape(-1)
    pick_rows = flat_ids * capacity + slot_index
    picker = token_picker(pick_rows, tok_dev, top_count, experts * capacity)
    row_grad = row_float.astype(jnp.bfloat16)
    returned = lax.all_to_all(
        row_grad.reshape(experts, capacity, width_dev),
        "expert",
        split_axis=0,
        concat_axis=0,
        tiled=True,
    )
    summed = jnp.dot(
        picker.astype(jnp.bfloat16),
        returned.reshape(experts * capacity, width_dev),
        preferred_element_type=jnp.float32,
    )
    token_grad = lax.psum_scatter(
        summed.astype(jnp.bfloat16), "section", scatter_dimension=1, tiled=True
    )
    down_wgrad = contract_rows(activated, grad_in).astype(jnp.bfloat16)[None]
    gate_wgrad = contract_rows(rows_in, gate_grad).astype(jnp.bfloat16)[None]
    up_wgrad = contract_rows(rows_in, up_grad).astype(jnp.bfloat16)[None]
    return (token_grad, gate_wgrad, up_wgrad, down_wgrad)


def solution(mesh):
    return jax.shard_map(
        on_device,
        mesh=mesh,
        in_specs=(
            P("expert", ("tp", "section")),
            P("expert", ("tp", "section")),
            P("expert", None),
            P("expert", None),
            P("expert", "tp", "section"),
            P("expert", "tp", "section"),
            P("expert", "section", "tp"),
        ),
        out_specs=(
            P("expert", ("tp", "section")),
            P("expert", "tp", "section"),
            P("expert", "tp", "section"),
            P("expert", "section", "tp"),
        ),
        check_vma=False,
    )
```

profile of v0, /device:TPU:0, one launch (start us, length us, event | category | flops | bytes accessed | tf_op | source)
XLA Modules:
  0.0 146.0 jit_solution(16408117409870252300)
XLA Ops:
  7.2 0.0 copy-start
  7.2 0.9 copy.20
  8.0 0.1 eq.55
  8.2 0.1 eq.51
  8.3 2.4 %all_gather.7 = bf16[128,1024]{1,0:T(8,128)(2,1)S(1)} all-gather(bf16[128,512]{1,0:T(8,128)(2,1)} %param.7), channel_id=1, replica_groups=mesh['section'=2,'expert'=4,'tp'=4] {'section'}, dimensions={1}, use_global_device_ids=true | all-gather | bytes 393216 | tf_op jit(solution)/shard_map/all_gather | solution.py:80
  10.7 1.2 reduce-window.6
  11.9 0.1 slice.10
  12.0 0.1 copy.23
  12.2 0.1 copy.24
  12.3 0.1 add_bitcast_fusion
  12.4 0.1 reduce_sum.23
  12.5 0.6 fusion.43
  13.2 0.1 mul.53
  13.3 1.4 scatter_custom_fusion
  14.7 0.1 reshape.145
  14.8 1.4 scatter_custom_fusion.1
  16.2 0.1 gt.11
  16.3 1.2 convolution_convert_fusion.3
  17.5 6.2 %all-to-all-start.1 = ((bf16[4,72,1024]{2,1,0:T(8,128)(2,1)}), bf16[4,72,1024]{2,1,0:T(8,128)(2,1)S(1)}, u32[]{:S(2)}, u32[]{:S(2)}) async-start(bf16[4,72,1024]{2,1,0:T(8,128)(2,1)} %convolution_convert_fusion.3), calls=%async_computation.1 | async-start | bytes 1179648 | tf_op jit(solution)/shard_map/all_to_all | solution.py:85
  23.7 0.1 reshape.147
  23.8 0.1 copy.26
  23.9 0.1 reshape.146
  24.1 0.1 reshape.154
  24.2 2.5 %gather_fusion = f32[288]{0:T(512)S(1)} fusion(f32[256]{0:T(256)S(1)} %reshape.146, s32[1024]{0:T(1024)S(1)} %pad_clamp_fusion), kind=kCustom, calls=%fused_computation | custom fusion | bytes 3456 | tf_op jit(solution)/shard_map/gather | solution.py:51
  26.6 0.1 reshape.153
  26.7 2.1 %all_gather.6 = bf16[128,1024]{1,0:T(8,128)(2,1)S(1)} all-gather(bf16[128,512]{1,0:T(8,128)(2,1)S(1)} %copy-done.4), channel_id=1, replica_groups=mesh['section'=2,'expert'=4,'tp'=4] {'section'}, dimensions={1}, use_global_device_ids=true | all-gather | bytes 393216 | tf_op jit(solution)/shard_map/all_gather | solution.py:81
  28.8 1.2 fusion.1
  30.0 9.9 %all-to-all-done.1 = bf16[4,72,1024]{2,1,0:T(8,128)(2,1)S(1)} async-done(((bf16[4,72,1024]{2,1,0:T(8,128)(2,1)}), bf16[4,72,1024]{2,1,0:T(8,128)(2,1)S(1)}, u32[]{:S(2)}, u32[]{:S(2)}) %all-to-all-start.1) | async-done | bytes 589856 | tf_op jit(solution)/shard_map/all_to_all | solution.py:85
  40.0 3.5 %all-to-all-start = ((bf16[4,72,1024]{2,1,0:T(8,128)(2,1)}), bf16[4,72,1024]{2,1,0:T(8,128)(2,1)S(1)}, u32[]{:S(2)}, u32[]{:S(2)}) async-start(bf16[4,72,1024]{2,1,0:T(8,128)(2,1)} %fusion.1), calls=%async_computation | async-start | bytes 1179648 | tf_op jit(solution)/shard_map/all_to_all | solution.py:86
  43.4 0.0 all-reduce.3.cloned.1.call-start
  43.5 1.2 convolution_convert_fusion.6
  44.7 14.2 %all-to-all-done = bf16[4,72,1024]{2,1,0:T(8,128)(2,1)S(1)} async-done(((bf16[4,72,1024]{2,1,0:T(8,128)(2,1)}), bf16[4,72,1024]{2,1,0:T(8,128)(2,1)S(1)}, u32[]{:S(2)}, u32[]{:S(2)}) %all-to-all-start) | async-done | bytes 589856 | tf_op jit(solution)/shard_map/all_to_all | solution.py:86
  58.9 1.2 convolution_convert_fusion.7
  60.0 1.2 convolution_convert_fusion.5
  61.2 0.0 all-reduce.3.cloned.1.call-update
  61.2 46.9 %all-reduce.3.cloned.1.call-done = (bf16[288,384]{1,0:T(8,128)(2,1)}, bf16[288,384]{1,0:T(8,128)(2,1)}, bf16[288,384]{1,0:T(8,128)(2,1)}) async-done(((bf16[288,384]{1,0:T(8,128)(2,1)}, bf16[288,384]{1,0:T(8,128)(2,1)}, bf16[288,384]{1,0:T(8,128)(2,1)}), (bf16[288,384]{1,0:T(8,128)(2,1)}, bf16[288,384]{1,0:T(8,128)(2,1)}, bf16[288,384]{1,0:T(8,128)(2,1)})) %all-reduce.3.cloned.1.call-update) | async-done | bytes 663568 | tf_op jit(solution)/shard_map/psum | solution.py:99
  108.1 1.8 %fusion.5 = f32[288,1024]{1,0:T(8,128)S(1)} fusion(bf16[1,1024,384]{2,1,0:T(8,128)(2,1)S(1)} %copy-done, bf16[288,384]{1,0:T(8,128)(2,1)} %get-tuple-element.4, bf16[288,384]{1,0:T(8,128)(2,1)} %get-tuple-element.5, bf16[288,384]{1,0:T(8,128)(2,1)} %get-tuple-element.6), kind=kOutput, calls=%fused_computation.18 | convolution fusion | flops 227930112 | bytes 2629632 | tf_op jit(solution)/shard_map/dot_general | solution.py:69
  109.9 1.3 fusion
  111.2 4.7 %all-to-all-start.2 = ((bf16[4,72,1024]{2,1,0:T(8,128)(2,1)}), bf16[4,72,1024]{2,1,0:T(8,128)(2,1)S(1)}, u32[]{:S(2)}, u32[]{:S(2)}) async-start(bf16[4,72,1024]{2,1,0:T(8,128)(2,1)} %bitcast.11), calls=%async_computation.2 | async-start | bytes 1179648 | tf_op jit(solution)/shard_map/all_to_all | solution.py:108
  116.0 0.1 copy.25
  116.0 0.1 convert_reduce_fusion
  116.1 15.8 %all-to-all-done.2 = bf16[4,72,1024]{2,1,0:T(8,128)(2,1)S(1)} async-done(((bf16[4,72,1024]{2,1,0:T(8,128)(2,1)}), bf16[4,72,1024]{2,1,0:T(8,128)(2,1)S(1)}, u32[]{:S(2)}, u32[]{:S(2)}) %all-to-all-start.2) | async-done | bytes 589856 | tf_op jit(solution)/shard_map/all_to_all | solution.py:108
  131.9 1.0 convolution_convert_fusion.4
  133.0 0.0 reduce-scatter.2.cloned.1.call-update
  133.0 1.6 %fusion.4 = bf16[1,384,1024]{2,1,0:T(8,128)(2,1)} fusion(bf16[288,1024]{1,0:T(8,128)(2,1)S(1)} %bitcast.64, bf16[288,384]{1,0:T(8,128)(2,1)S(1)} %copy-done.6, bf16[288,384]{1,0:T(8,128)(2,1)S(1)} %copy-done.8), kind=kOutput, calls=%fused_computation.13 | convolution fusion | flops 227770368 | bytes 1818624 | tf_op jit(solution)/shard_map/dot_general | solution.py:63
  134.5 1.6 %fusion.3 = bf16[1,1024,384]{2,1,0:T(8,128)(2,1)} fusion(bf16[288,1024]{1,0:T(8,128)(2,1)S(1)} %bitcast.61, bf16[288,384]{1,0:T(8,128)(2,1)S(1)} %copy-done.8, bf16[288,384]{1,0:T(8,128)(2,1)S(1)} %copy-done.7), kind=kOutput, calls=%fused_computation.12 | convolution fusion | flops 227770368 | bytes 1818624 | tf_op jit(solution)/shard_map/dot_general | solution.py:63
  136.2 1.7 %fusion.2 = bf16[1,1024,384]{2,1,0:T(8,128)(2,1)} fusion(bf16[288,1024]{1,0:T(8,128)(2,1)S(1)} %bitcast.62, bf16[288,384]{1,0:T(8,128)(2,1)S(1)} %copy-done.6, bf16[288,384]{1,0:T(8,128)(2,1)S(1)} %copy-done.7, bf16[288,384]{1,0:T(8,128)(2,1)S(1)} %copy-done.8), kind=kOutput, calls=%fused_computation.11 | convolution fusion | flops 228323328 | bytes 2039808 | tf_op jit(solution)/shard_map/dot_general | solution.py:63
  137.8 1.4 reduce-scatter.2.cloned.1.call-done
  (29 shorter events, 0.1 us)
Async XLA Ops:
  7.2 52.9 %copy-start = (bf16[1,1024,384]{2,1,0:T(8,128)(2,1)S(1)}, bf16[1,1024,384]{2,1,0:T(8,128)(2,1)}, u32[]{:S(2)}) copy-start(bf16[1,1024,384]{2,1,0:T(8,128)(2,1)} %param.11) | copy-start | bytes 2359300
  12.5 11.3 %copy-start.5 = (f32[128,2]{0,1:T(2,128)S(1)}, f32[128,2]{0,1:T(2,128)}, u32[]{:S(2)}) copy-start(f32[128,2]{0,1:T(2,128)} %param.10) | copy-start | bytes 3076
  17.5 22.4 %all-to-all-start.1 = ((bf16[4,72,1024]{2,1,0:T(8,128)(2,1)}), bf16[4,72,1024]{2,1,0:T(8,128)(2,1)S(1)}, u32[]{:S(2)}, u32[]{:S(2)}) async-start(bf16[4,72,1024]{2,1,0:T(8,128)(2,1)} %convolution_convert_fusion.3), calls=%async_computation.1 | async-start | bytes 1179648 | tf_op jit(solution)/shard_map/all_to_all | solution.py:85
  23.7 3.0 %copy-start.4 = (bf16[128,512]{1,0:T(8,128)(2,1)S(1)}, bf16[128,512]{1,0:T(8,128)(2,1)}, u32[]{:S(2)}) copy-start(bf16[128,512]{1,0:T(8,128)(2,1)} %param.8) | copy-start | bytes 393220
  26.7 16.8 %copy-start.2 = (bf16[1,1024,384]{2,1,0:T(8,128)(2,1)S(1)}, bf16[1,1024,384]{2,1,0:T(8,128)(2,1)}, u32[]{:S(2)}) copy-start(bf16[1,1024,384]{2,1,0:T(8,128)(2,1)} %param.12) | copy-start | bytes 2359300
  30.0 28.8 %copy-start.1 = (bf16[1,384,1024]{2,1,0:T(8,128)(2,1)S(1)}, bf16[1,384,1024]{2,1,0:T(8,128)(2,1)}, u32[]{:S(2)}) copy-start(bf16[1,384,1024]{2,1,0:T(8,128)(2,1)} %param.13) | copy-start | bytes 2359300
  40.0 18.9 %all-to-all-start = ((bf16[4,72,1024]{2,1,0:T(8,128)(2,1)}), bf16[4,72,1024]{2,1,0:T(8,128)(2,1)S(1)}, u32[]{:S(2)}, u32[]{:S(2)}) async-start(bf16[4,72,1024]{2,1,0:T(8,128)(2,1)} %fusion.1), calls=%async_computation | async-start | bytes 1179648 | tf_op jit(solution)/shard_map/all_to_all | solution.py:86
  43.4 64.7 %all-reduce.3.cloned.1.call-start = ((), (), s32[]{:S(2)}) async-start(), calls=%async_computation.5 | async-start | bytes 1327104 | tf_op jit(solution)/shard_map/psum | solution.py:99
  108.1 1.8 %copy-start.7 = (bf16[288,384]{1,0:T(8,128)(2,1)S(1)}, bf16[288,384]{1,0:T(8,128)(2,1)}, u32[]{:S(2)}) copy-start(bf16[288,384]{1,0:T(8,128)(2,1)} %get-tuple-element.5) | copy-start | bytes 663556
  108.1 1.8 %copy-start.8 = (bf16[288,384]{1,0:T(8,128)(2,1)S(1)}, bf16[288,384]{1,0:T(8,128)(2,1)}, u32[]{:S(2)}) copy-start(bf16[288,384]{1,0:T(8,128)(2,1)} %get-tuple-element.6) | copy-start | bytes 663556
  111.2 4.7 %copy-start.3 = (s32[128,2]{1,0:T(8,128)S(1)}, s32[128,2]{1,0:T(8,128)}, u32[]{:S(2)}) copy-start(s32[128,2]{1,0:T(8,128)} %get-tuple-element.7) | copy-start | bytes 3076
  111.2 21.8 %copy-start.6 = (bf16[288,384]{1,0:T(8,128)(2,1)S(1)}, bf16[288,384]{1,0:T(8,128)(2,1)}, u32[]{:S(2)}) copy-start(bf16[288,384]{1,0:T(8,128)(2,1)} %get-tuple-element.4) | copy-start | bytes 663556
  111.2 20.7 %all-to-all-start.2 = ((bf16[4,72,1024]{2,1,0:T(8,128)(2,1)}), bf16[4,72,1024]{2,1,0:T(8,128)(2,1)S(1)}, u32[]{:S(2)}, u32[]{:S(2)}) async-start(bf16[4,72,1024]{2,1,0:T(8,128)(2,1)} %bitcast.11), calls=%async_computation.2 | async-start | bytes 1179648 | tf_op jit(solution)/shard_map/all_to_all | solution.py:108
  116.0 23.2 %reduce-scatter.2.cloned.1.call-start = ((), (), s32[]{:S(2)}) async-start(), calls=%async_computation.4 | async-start | bytes 393216 | tf_op jit(solution)/shard_map/reduce_scatter | solution.py:120
Sparse Core Ops, SparseCore 0:
  61.3 46.7 all-reduce.2
  133.1 6.0 reduce-scatter.1
where the time goes:
time: 146 us
  waiting for transfers between devices  88.2 us (60%)
  matrix products  14.8 us (10%)
  starting transfers between devices  14.5 us (10%)
  between operations  14.2 us (10%)
  local copies, waits for them, and re-layouts  7.71 us (5%)
  blocking collectives  4.53 us (3%)
  other arithmetic  2.08 us (1%)
    psum x1, waiting for transfers between devices, on_device(): lax.psum(up_part.astype(jnp.bfloat16), 'tp').astype(jnp.float32)  46.9 us
    all_to_all x1, waiting for transfers between devices, on_device(): lax.all_to_all(row_grad.reshape(experts, capacity, width_dev), 'expert',...  15.8 us
    all_to_all x1, waiting for transfers between devices, on_device(): lax.all_to_all(send_grads, 'expert', split_axis=0, concat_axis=0, tiled=T...  14.2 us
    all_to_all x1, waiting for transfers between devices, on_device(): lax.all_to_all(send_rows, 'expert', split_axis=0, concat_axis=0, tiled=True)  9.92 us
    all_to_all x1, starting transfers between devices, on_device(): lax.all_to_all(send_rows, 'expert', split_axis=0, concat_axis=0, tiled=True)  6.21 us
    dot_general x3, matrix products, contract_rows(): lax.dot_general(left_side, right_side, (((0,), (0,)), ((), ())), preferre...  4.83 us
    all_to_all x1, starting transfers between devices, on_device(): lax.all_to_all(row_grad.reshape(experts, capacity, width_dev), 'expert',...  4.74 us
    dot_general x3, matrix products, contract_last(): lax.dot_general(left_side, right_side, (((1,), (1,)), ((), ())), preferre...  4.27 us
  transfers between devices with their start and end apart: 5, of which 5 were waited for; matrix products, arithmetic and copies ran while one was open for 7% of the time, Pallas kernels for 0%

commit v1 on v0

--- a/solution.py
+++ b/solution.py
@@ -1,7 +1,13 @@
+import functools
+
 import jax
 import jax.numpy as jnp
 from jax import lax
+from jax.experimental import pallas as pl
+from jax.experimental.pallas import tpu as pltpu
 from jax.sharding import PartitionSpec as P
+
+MESH = pl.DeviceIdType.MESH
 
 
 def block_slots(expert_ids, experts, capacity):
@@ -126,9 +132,355 @@
     return (token_grad, gate_wgrad, up_wgrad, down_wgrad)
 
 
+def expert_kernel(
+    n,
+    slots,
+    tok_ref,
+    grad_ref,
+    ids_ref,
+    combine_ref,
+    gate_hbm,
+    up_hbm,
+    down_hbm,
+    token_out,
+    gate_out,
+    up_out,
+    down_out,
+    gate_w,
+    up_w,
+    down_w,
+    picks,
+    send_rows,
+    send_grads,
+    rows,
+    grads,
+    parts,
+    got_parts,
+    local,
+    halves,
+    got_half,
+    back,
+    returned,
+    gate_g,
+    up_g,
+    down_g,
+    io_sem,
+    z_send,
+    z_recv,
+    s_send,
+    s_recv,
+    p_send,
+    p_recv,
+    a_send,
+    a_recv,
+    h_send,
+    h_recv,
+    r_send,
+    r_recv,
+):
+    sec = lax.axis_index("section")
+    exp = lax.axis_index("expert")
+    tp = lax.axis_index("tp")
+    other = 1 - sec
+    tok_dev, width = tok_ref.shape
+    hidden = gate_w.shape[1]
+
+    def hop(axis, index):
+        place = {"section": sec, "expert": exp, "tp": tp}
+        place[axis] = index
+        return (place["section"], place["expert"], place["tp"])
+
+    def remote(src, dst, send, recv, target):
+        return pltpu.make_async_remote_copy(
+            src_ref=src,
+            dst_ref=dst,
+            send_sem=send,
+            recv_sem=recv,
+            device_id=target,
+            device_id_type=MESH,
+        )
+
+    loads = [
+        pltpu.make_async_copy(src, dst, io_sem.at[index])
+        for index, (src, dst) in enumerate(((gate_hbm, gate_w), (up_hbm, up_w), (down_hbm, down_w)))
+    ]
+    for load in loads:
+        load.start()
+
+    barrier = pltpu.get_barrier_semaphore()
+    pl.semaphore_signal(barrier, inc=1, device_id=hop("section", other), device_id_type=MESH)
+    for step in range(1, n):
+        pl.semaphore_signal(
+            barrier, inc=1, device_id=hop("expert", lax.rem(exp + step, n)), device_id_type=MESH
+        )
+        pl.semaphore_signal(
+            barrier, inc=1, device_id=hop("tp", lax.rem(tp + step, n)), device_id_type=MESH
+        )
+
+    target = lax.rem(exp + lax.broadcasted_iota(jnp.int32, (tok_dev, 128), 1), n)
+    first = ids_ref[:, 0:1] == target
+    second = ids_ref[:, 1:2] == target
+    named = jnp.logical_or(first, second).astype(jnp.float32)
+    weight = jnp.where(first, combine_ref[:, 0:1], 0.0) + jnp.where(second, combine_ref[:, 1:2], 0.0)
+    earlier = (
+        lax.broadcasted_iota(jnp.int32, (tok_dev, tok_dev), 1)
+        < lax.broadcasted_iota(jnp.int32, (tok_dev, tok_dev), 0)
+    ).astype(jnp.bfloat16)
+    slot = jnp.dot(earlier, named.astype(jnp.bfloat16), preferred_element_type=jnp.float32)
+    place = jnp.where(named > 0.0, slot, -1.0)
+    columns = lax.broadcasted_iota(jnp.int32, (tok_dev, slots), 1).astype(jnp.float32)
+    tokens = tok_ref[...]
+    out_grad = grad_ref[...].astype(jnp.float32)
+
+    def block(d):
+        return pl.ds(d * slots, slots)
+
+    def z_copies(d):
+        goal = hop("expert", lax.rem(exp + d, n))
+        return (
+            remote(send_rows.at[d - 1], rows.at[sec, block(d)], z_send.at[0, d - 1], z_recv.at[0, d - 1], goal),
+            remote(send_grads.at[d - 1], grads.at[sec, block(d)], z_send.at[1, d - 1], z_recv.at[1, d - 1], goal),
+        )
+
+    def s_copies(d):
+        goal = hop("section", other)
+        return (
+            remote(rows.at[sec, block(d)], rows.at[sec, block(d)], s_send.at[0, d], s_recv.at[0, d], goal),
+            remote(grads.at[sec, block(d)], grads.at[sec, block(d)], s_send.at[1, d], s_recv.at[1, d], goal),
+        )
+
+    order = [2, 1, 3, 0] if n == 4 else list(range(1, n)) + [0]
+    for turn, d in enumerate(order):
+        pick = (place[:, d : d + 1] == columns).astype(jnp.bfloat16)
+        picks[d] = pick
+        picked = contract_rows(pick, tokens).astype(jnp.bfloat16)
+        scaled = (out_grad * weight[:, d : d + 1]).astype(jnp.bfloat16)
+        picked_grad = contract_rows(pick, scaled).astype(jnp.bfloat16)
+        if d == 0:
+            rows[sec, block(0)] = picked
+            grads[sec, block(0)] = picked_grad
+            for copy in s_copies(0):
+                copy.start()
+        else:
+            send_rows[d - 1] = picked
+            send_grads[d - 1] = picked_grad
+            if turn == 0:
+                pl.semaphore_wait(barrier, 2 * n - 1)
+            for copy in z_copies(d):
+                copy.start()
+
+    for load in loads:
+        load.wait()
+
+    def p_copy(d):
+        slot_there = lax.rem(tp - d + n, n) - 1
+        return remote(
+            parts.at[d], got_parts.at[slot_there], p_send.at[d], p_recv.at[slot_there], hop("tp", d)
+        )
+
+    arrivals = [0, 1, 3, 2] if n == 4 else list(range(n))
+    for d in arrivals:
+        if d != 0:
+            for copy, onward in zip(z_copies(d), s_copies(d)):
+                copy.wait_recv()
+                onward.start()
+        for copy in s_copies(d):
+            copy.wait_recv()
+        for index, weights in ((0, gate_w), (1, up_w)):
+            total = jnp.dot(rows[0, block(d)], weights[0:width, :], preferred_element_type=jnp.float32)
+            total += jnp.dot(rows[1, block(d)], weights[width : 2 * width, :], preferred_element_type=jnp.float32)
+            parts[d, :, index * hidden : (index + 1) * hidden] = total.astype(jnp.bfloat16)
+        total = contract_last(grads[0, block(d)], down_w[:, 0:width])
+        total += contract_last(grads[1, block(d)], down_w[:, width : 2 * width])
+        parts[d, :, 2 * hidden : 3 * hidden] = total.astype(jnp.bfloat16)
+
+        @pl.when(tp != d)
+        def _():
+            p_copy(d).start()
+
+    def p_arrival(k):
+        return remote(parts.at[0], got_parts.at[k], p_send.at[0], p_recv.at[k], hop("tp", lax.rem(tp + 1, n)))
+
+    summed = parts[tp].astype(jnp.float32)
+    for k in range(n - 1):
+        p_arrival(k).wait_recv()
+        summed += got_parts[k].astype(jnp.float32)
+    activated, gate_grad, up_grad = local_grads(
+        summed[:, 0:hidden], summed[:, hidden : 2 * hidden], summed[:, 2 * hidden : 3 * hidden]
+    )
+    local[tp, :, 0:hidden] = gate_grad
+    local[tp, :, hidden : 2 * hidden] = up_grad
+    local[tp, :, 2 * hidden : 3 * hidden] = activated
+
+    def a_copy(k):
+        return remote(
+            local.at[tp], local.at[tp], a_send.at[k - 1], a_recv.at[k - 1], hop("tp", lax.rem(tp + k, n))
+        )
+
+    for k in (2, 1, 3) if n == 4 else range(1, n):
+        a_copy(k).start()
+
+    def h_copy(k):
+        return remote(halves.at[k], got_half.at[k], h_send.at[k], h_recv.at[k], hop("section", other))
+
+    def r_copy(k, p):
+        return remote(
+            back.at[k],
+            returned.at[p],
+            r_send.at[k],
+            r_recv.at[p],
+            hop("expert", lax.rem(exp - p + n, n)),
+        )
+
+    for k in (0, 1, 3, 2) if n == 4 else range(n):
+        p = lax.rem(tp - k + n, n)
+        if k > 0:
+            a_copy(k).wait_recv()
+        gate_grad = local[p, :, 0:hidden]
+        up_grad = local[p, :, hidden : 2 * hidden]
+
+        def row_part(side):
+            span = pl.ds(pl.multiple_of(side * width, width), width)
+            total = contract_last(gate_grad, gate_w[span, :])
+            return total + contract_last(up_grad, up_w[span, :])
+
+        halves[k] = row_part(other).astype(jnp.bfloat16)
+        h_copy(k).start()
+        own = row_part(sec)
+        h_copy(k).wait_recv()
+        whole = (own + got_half[k].astype(jnp.float32)).astype(jnp.bfloat16)
+
+        @pl.when(p == 0)
+        def _():
+            returned[0] = whole
+
+        @pl.when(p != 0)
+        def _():
+            back[k] = whole
+            r_copy(k, p).start()
+
+    total_rows = n * slots
+    every = local[...].reshape(total_rows, 3 * hidden)
+    chunk = 256
+    stores = []
+    for index, (result, out) in enumerate(((gate_g, gate_out), (up_g, up_out))):
+        for side in range(2):
+            for low in range(0, width, chunk):
+                left = rows[side, :, low : low + chunk]
+                start = side * width + low
+                result[start : start + chunk, :] = sum(contract_rows(rows[side, block(d), low : low + chunk], local[d, :, index * hidden : (index + 1) * hidden]) for d in range(n)).astype(jnp.bfloat16)
+        store = pltpu.make_async_copy(result, out, io_sem.at[3 + index])
+        store.start()
+        stores.append(store)
+    right = every[:, 2 * hidden : 3 * hidden]
+    for side in range(2):
+        for low in range(0, width, chunk):
+            start = side * width + low
+            down_g[:, start : start + chunk] = contract_rows(
+                right, grads[side, :, low : low + chunk]
+            ).astype(jnp.bfloat16)
+    store = pltpu.make_async_copy(down_g, down_out, io_sem.at[5])
+    store.start()
+    stores.append(store)
+
+    total = jnp.dot(picks[0], returned[0], preferred_element_type=jnp.float32)
+    for d in (1, 3, 2) if n == 4 else range(1, n):
+        remote(back.at[0], returned.at[d], r_send.at[0], r_recv.at[d], hop("expert", lax.rem(exp + 1, n))).wait_recv()
+        total += jnp.dot(picks[d], returned[d], preferred_element_type=jnp.float32)
+    token_out[...] = total.astype(jnp.bfloat16)
+
+    for d in range(1, n):
+        for copy in z_copies(d):
+            copy.wait_send()
+        a_copy(d).wait_send()
+    for d in range(n):
+        for copy in s_copies(d):
+            copy.wait_send()
+        h_copy(d).wait_send()
+
+        @pl.when(tp != d)
+        def _():
+            p_copy(d).wait_send()
+
+        p = lax.rem(tp - d + n, n)
+
+        @pl.when(p != 0)
+        def _():
+            r_copy(d, p).wait_send()
+
+    for store in stores:
+        store.wait()
+
+
+def on_device_kernel(tokens, out_grad, expert_ids, combine, w_gate, w_up, w_down):
+    tok_dev, top_count = expert_ids.shape
+    n = lax.axis_size("expert")
+    capacity = (tok_dev * top_count * 9 + 8 * n - 1) // (8 * n)
+    slots = (capacity + 15) // 16 * 16
+    width = tokens.shape[1]
+    depth, hidden = w_gate.shape[1:]
+    bf16 = jnp.bfloat16
+    vmem = pl.BlockSpec(memory_space=pltpu.VMEM)
+    hbm = pl.BlockSpec(memory_space=pl.ANY)
+    dma = pltpu.SemaphoreType.DMA
+    token_grad, gate_g, up_g, down_g = pl.pallas_call(
+        functools.partial(expert_kernel, n, slots),
+        out_shape=(
+            jax.ShapeDtypeStruct((tok_dev, width), bf16),
+            jax.ShapeDtypeStruct((depth, hidden), bf16),
+            jax.ShapeDtypeStruct((depth, hidden), bf16),
+            jax.ShapeDtypeStruct((hidden, depth), bf16),
+        ),
+        in_specs=[vmem, vmem, vmem, vmem, hbm, hbm, hbm],
+        out_specs=(vmem, hbm, hbm, hbm),
+        scratch_shapes=[
+            pltpu.VMEM((depth, hidden), bf16),
+            pltpu.VMEM((depth, hidden), bf16),
+            pltpu.VMEM((hidden, depth), bf16),
+            pltpu.VMEM((n, tok_dev, slots), bf16),
+            pltpu.VMEM((n - 1, slots, width), bf16),
+            pltpu.VMEM((n - 1, slots, width), bf16),
+            pltpu.VMEM((2, n * slots, width), bf16),
+            pltpu.VMEM((2, n * slots, width), bf16),
+            pltpu.VMEM((n, slots, 3 * hidden), bf16),
+            pltpu.VMEM((n - 1, slots, 3 * hidden), bf16),
+            pltpu.VMEM((n, slots, 3 * hidden), bf16),
+            pltpu.VMEM((n, slots, width), bf16),
+            pltpu.VMEM((n, slots, width), bf16),
+            pltpu.VMEM((n, slots, width), bf16),
+            pltpu.VMEM((n, slots, width), bf16),
+            pltpu.VMEM((depth, hidden), bf16),
+            pltpu.VMEM((depth, hidden), bf16),
+            pltpu.VMEM((hidden, depth), bf16),
+            dma((6,)),
+            dma((2, n - 1)),
+            dma((2, n - 1)),
+            dma((2, n)),
+            dma((2, n)),
+            dma((n,)),
+            dma((n - 1,)),
+            dma((n - 1,)),
+            dma((n - 1,)),
+            dma((n,)),
+            dma((n,)),
+            dma((n,)),
+            dma((n,)),
+        ],
+        compiler_params=pltpu.CompilerParams(
+            collective_id=0, has_side_effects=True, vmem_limit_bytes=48 * 1024 * 1024
+        ),
+    )(tokens, out_grad, expert_ids, combine, w_gate[0], w_up[0], w_down[0])
+    return (token_grad, gate_g[None], up_g[None], down_g[None])
+
+
+def fits_kernel(mesh):
+    shape = mesh.shape
+    return shape["section"] == 2 and shape["expert"] == shape["tp"]
+
+
 def solution(mesh):
     return jax.shard_map(
-        on_device,
+        on_device_kernel if fits_kernel(mesh) else on_device,
         mesh=mesh,
         in_specs=(
             P("expert", ("tp", "section")),

time: 146 us -> 63.2 us (0.43)
  the two profiles are of different devices: /device:TPU:0 before, /device:TPU:19 now
where the time goes in v1:
time: 63.2 us; the launch traced here: 62.9 us
  Pallas kernels  53 us (84%)
  local copies, waits for them, and re-layouts  9.2 us (15%)
  between operations  0.66 us (1%)
    pallas_call x1, Pallas kernels, on_device_kernel(): pl.pallas_call(functools.partial(expert_kernel, n, slots), out_shape=(jax...  53 us
    unnamed x16, local copies, waits for them, and re-layouts  9.2 us

profile of v1, /device:TPU:19, one launch (start us, length us, event | category | flops | bytes accessed | tf_op | source)
XLA Modules:
  0.0 62.9 jit_solution(14959591987927281308)
XLA Ops:
  0.6 0.0 copy-start.3
  0.6 0.8 %copy.11.ids_ref = s32[128,2]{1,0:T(8,128)S(1)} copy(s32[128,2]{0,1:T(2,128)} %param.9) | data formatting | bytes 2048 | tf_op args[2]
  1.5 0.8 %copy.12.combine_ref = f32[128,2]{1,0:T(8,128)S(1)} copy(f32[128,2]{0,1:T(2,128)} %param.10) | data formatting | bytes 2048 | tf_op args[3]
  2.2 0.0 copy-done.3
  2.2 0.0 copy-start
  2.3 1.1 %copy-done = bf16[1,1024,384]{2,1,0:T(8,128)(2,1)S(1)} copy-done((bf16[1,1024,384]{2,1,0:T(8,128)(2,1)S(1)}, bf16[1,1024,384]{2,1,0:T(8,128)(2,1)}, u32[]{:S(2)}) %copy-start) | copy-done | bytes 786456
  3.4 0.0 copy-start.1
  3.4 1.1 %copy-done.1 = bf16[1,1024,384]{2,1,0:T(8,128)(2,1)S(1)} copy-done((bf16[1,1024,384]{2,1,0:T(8,128)(2,1)S(1)}, bf16[1,1024,384]{2,1,0:T(8,128)(2,1)}, u32[]{:S(2)}) %copy-start.1) | copy-done | bytes 786456
  4.5 0.0 copy-start.2
  4.5 1.1 %copy-done.2 = bf16[1,384,1024]{2,1,0:T(8,128)(2,1)S(1)} copy-done((bf16[1,384,1024]{2,1,0:T(8,128)(2,1)S(1)}, bf16[1,384,1024]{2,1,0:T(8,128)(2,1)}, u32[]{:S(2)}) %copy-start.2) | copy-done | bytes 786456
  5.7 0.0 copy-start.4
  5.7 0.9 %copy-done.4 = bf16[128,512]{1,0:T(8,128)(2,1)S(1)} copy-done((bf16[128,512]{1,0:T(8,128)(2,1)S(1)}, bf16[128,512]{1,0:T(8,128)(2,1)}, u32[]{:S(2)}) %copy-start.4) | copy-done | bytes 131096
  6.6 53.0 %shard_map.102 = (bf16[128,512]{1,0:T(8,128)(2,1)S(1)}, bf16[1024,384]{1,0:T(8,128)(2,1)S(1)}, bf16[1024,384]{1,0:T(8,128)(2,1)S(1)}, bf16[384,1024]{1,0:T(8,128)(2,1)S(1)}) custom-call(bf16[128,512]{1,0:T(8,128)(2,1)S(1)} %copy-done.3, bf16[128,512]{1,0:T(8,128)(2,1)S(1)} %copy-done.4, s32[128,2]{1,0:T(8,128)S(1)} %copy.11.ids_ref, ...), custom_call_target="tpu_custom_call" | custom-call | tf_op jit(solution)/shard_map/pallas_call | solution.py:426
  59.6 0.7 %copy.17 = bf16[128,512]{1,0:T(8,128)(2,1)} copy(bf16[128,512]{1,0:T(8,128)(2,1)S(1)} %get-tuple-element.16) | data formatting | bytes 262144
  60.2 0.9 %copy.18 = bf16[1,1024,384]{2,1,0:T(8,128)(2,1)} copy(bf16[1,1024,384]{2,1,0:T(8,128)(2,1)S(1)} %bitcast.8) | data formatting | bytes 1572864
  61.1 0.9 %copy.19 = bf16[1,1024,384]{2,1,0:T(8,128)(2,1)} copy(bf16[1,1024,384]{2,1,0:T(8,128)(2,1)S(1)} %bitcast.7) | data formatting | bytes 1572864
  62.0 0.9 %copy.20 = bf16[1,384,1024]{2,1,0:T(8,128)(2,1)} copy(bf16[1,384,1024]{2,1,0:T(8,128)(2,1)S(1)} %bitcast.6) | data formatting | bytes 1572864
Async XLA Ops:
  0.6 1.6 %copy-start.3 = (bf16[128,512]{1,0:T(8,128)(2,1)S(1)}, bf16[128,512]{1,0:T(8,128)(2,1)}, u32[]{:S(2)}) copy-start(bf16[128,512]{1,0:T(8,128)(2,1)} %tok_ref.1) | copy-start | bytes 393220
  2.2 1.1 %copy-start = (bf16[1,1024,384]{2,1,0:T(8,128)(2,1)S(1)}, bf16[1,1024,384]{2,1,0:T(8,128)(2,1)}, u32[]{:S(2)}) copy-start(bf16[1,1024,384]{2,1,0:T(8,128)(2,1)} %param.11) | copy-start | bytes 2359300
  3.4 1.1 %copy-start.1 = (bf16[1,1024,384]{2,1,0:T(8,128)(2,1)S(1)}, bf16[1,1024,384]{2,1,0:T(8,128)(2,1)}, u32[]{:S(2)}) copy-start(bf16[1,1024,384]{2,1,0:T(8,128)(2,1)} %param.12) | copy-start | bytes 2359300
  4.5 1.1 %copy-start.2 = (bf16[1,384,1024]{2,1,0:T(8,128)(2,1)S(1)}, bf16[1,384,1024]{2,1,0:T(8,128)(2,1)}, u32[]{:S(2)}) copy-start(bf16[1,384,1024]{2,1,0:T(8,128)(2,1)} %param.13) | copy-start | bytes 2359300
  5.7 0.9 %copy-start.4 = (bf16[128,512]{1,0:T(8,128)(2,1)S(1)}, bf16[128,512]{1,0:T(8,128)(2,1)}, u32[]{:S(2)}) copy-start(bf16[128,512]{1,0:T(8,128)(2,1)} %grad_ref.1) | copy-start | bytes 393220

commit v2 on v0

--- a/solution.py
+++ b/solution.py
@@ -1,7 +1,13 @@
+import functools
+
 import jax
 import jax.numpy as jnp
 from jax import lax
+from jax.experimental import pallas as pl
+from jax.experimental.pallas import tpu as pltpu
 from jax.sharding import PartitionSpec as P
+
+MESH = pl.DeviceIdType.MESH
 
 
 def block_slots(expert_ids, experts, capacity):
@@ -126,9 +132,388 @@
     return (token_grad, gate_wgrad, up_wgrad, down_wgrad)
 
 
+def expert_kernel(
+    n,
+    slots,
+    tok_hbm,
+    grad_hbm,
+    ids_ref,
+    combine_ref,
+    gate_hbm,
+    up_hbm,
+    down_hbm,
+    token_out,
+    gate_out,
+    up_out,
+    down_out,
+    tok_ref,
+    grad_ref,
+    both_w,
+    down_w,
+    picks,
+    send_rows,
+    send_grads,
+    rows,
+    grads,
+    parts,
+    got_parts,
+    local,
+    halves,
+    got_half,
+    back,
+    returned,
+    gate_g,
+    up_g,
+    down_g,
+    io_sem,
+    z_send,
+    z_recv,
+    s_send,
+    s_recv,
+    p_send,
+    p_recv,
+    a_send,
+    a_recv,
+    h_send,
+    h_recv,
+    r_send,
+    r_recv,
+):
+    sec = lax.axis_index("section")
+    exp = lax.axis_index("expert")
+    tp = lax.axis_index("tp")
+    other = 1 - sec
+    tok_dev, width = tok_ref.shape
+    hidden = down_w.shape[0]
+    groups = hidden // 128
+    share = parts.shape[1] // n
+    sign = 2 * lax.rem(exp, 2) - 1
+
+    def hop(axis, index):
+        place = {"section": sec, "expert": exp, "tp": tp}
+        place[axis] = index
+        return (place["section"], place["expert"], place["tp"])
+
+    def remote(src, dst, send, recv, target):
+        return pltpu.make_async_remote_copy(
+            src_ref=src,
+            dst_ref=dst,
+            send_sem=send,
+            recv_sem=recv,
+            device_id=target,
+            device_id_type=MESH,
+        )
+
+    def partner(k):
+        return lax.rem(exp + n + sign * k, n)
+
+    fetch = [
+        pltpu.make_async_copy(tok_hbm, tok_ref, io_sem.at[0]),
+        pltpu.make_async_copy(grad_hbm, grad_ref, io_sem.at[1]),
+    ]
+    loads = [pltpu.make_async_copy(down_hbm, down_w, io_sem.at[2])]
+    for j in range(groups):
+        for index, source in enumerate((gate_hbm, up_hbm)):
+            loads.append(
+                pltpu.make_async_copy(
+                    source.at[:, pl.ds(j * 128, 128)],
+                    both_w.at[:, pl.ds((2 * j + index) * 128, 128)],
+                    io_sem.at[3 + 2 * j + index],
+                )
+            )
+    for copy in fetch + loads:
+        copy.start()
+
+    barrier = pltpu.get_barrier_semaphore()
+    pl.semaphore_signal(barrier, inc=1, device_id=hop("section", other), device_id_type=MESH)
+    for k in range(1, n):
+        pl.semaphore_signal(barrier, inc=1, device_id=hop("expert", partner(k)), device_id_type=MESH)
+        pl.semaphore_signal(
+            barrier, inc=1, device_id=hop("tp", lax.rem(tp + k, n)), device_id_type=MESH
+        )
+
+    target = lax.rem(exp + 2 * n + sign * lax.rem(lax.broadcasted_iota(jnp.int32, (8, tok_dev), 0), n), n)
+    first = ids_ref[0:1, :] == target
+    second = ids_ref[1:2, :] == target
+    named = jnp.logical_or(first, second).astype(jnp.float32)
+    weight = jnp.where(first, combine_ref[0:1, :], 0.0) + jnp.where(second, combine_ref[1:2, :], 0.0)
+    earlier = (
+        lax.broadcasted_iota(jnp.int32, (tok_dev, tok_dev), 0)
+        < lax.broadcasted_iota(jnp.int32, (tok_dev, tok_dev), 1)
+    ).astype(jnp.bfloat16)
+    slot = jnp.dot(named.astype(jnp.bfloat16), earlier, preferred_element_type=jnp.float32)
+    place = jnp.where(named > 0.0, slot, -1.0)
+    numbers = lax.broadcasted_iota(jnp.int32, (slots, tok_dev), 0).astype(jnp.float32)
+    spare = n * share - groups * slots
+    if spare > 0:
+        for k in range(n):
+            parts[k, groups * slots :, :] = jnp.zeros((spare, 384), jnp.bfloat16)
+
+    def block(k):
+        return pl.ds(k * slots, slots)
+
+    def z_copies(k):
+        goal = hop("expert", partner(k))
+        return (
+            remote(send_rows.at[k - 1], rows.at[sec, block(k)], z_send.at[0, k - 1], z_recv.at[0, k - 1], goal),
+            remote(send_grads.at[k - 1], grads.at[sec, block(k)], z_send.at[1, k - 1], z_recv.at[1, k - 1], goal),
+        )
+
+    def s_copies(k):
+        goal = hop("section", other)
+        return (
+            remote(rows.at[sec, block(k)], rows.at[sec, block(k)], s_send.at[0, k], s_recv.at[0, k], goal),
+            remote(grads.at[sec, block(k)], grads.at[sec, block(k)], s_send.at[1, k], s_recv.at[1, k], goal),
+        )
+
+    def p_copy(k, r):
+        goal = lax.rem(tp + r, n)
+        span = pl.ds(pl.multiple_of(goal * share, share), share)
+        return remote(
+            parts.at[k, span], got_parts.at[k, r - 1], p_send.at[k, r - 1], p_recv.at[k, r - 1], hop("tp", goal)
+        )
+
+    mine = pl.ds(pl.multiple_of(tp * share, share), share)
+
+    def a_copy(k, r):
+        return remote(
+            local.at[k, mine], local.at[k, mine], a_send.at[k, r - 1], a_recv.at[k, r - 1], hop("tp", lax.rem(tp + r, n))
+        )
+
+    def h_copy(k):
+        return remote(halves.at[k], got_half.at[k], h_send.at[k], h_recv.at[k], hop("section", other))
+
+    def r_copy(k):
+        return remote(back.at[k - 1], returned.at[k], r_send.at[k - 1], r_recv.at[k - 1], hop("expert", partner(k)))
+
+    far_first = (2, 1, 3)
+
+    for copy in fetch:
+        copy.wait()
+    for turn, k in enumerate((1, 2, 0, 3)):
+        pick = (place[k : k + 1, :] == numbers).astype(jnp.float32)
+        spread = jnp.sum(pick * weight[k : k + 1, :], axis=1, keepdims=True)
+        pick = pick.astype(jnp.bfloat16)
+        picks[k] = pick
+        picked = jnp.dot(pick, tok_ref[...], preferred_element_type=jnp.float32).astype(jnp.bfloat16)
+        if k == 0:
+            rows[sec, block(0)] = picked
+        else:
+            send_rows[k - 1] = picked
+            if turn == 0:
+                pl.semaphore_wait(barrier, 2 * n - 1)
+            z_copies(k)[0].start()
+        picked_grad = jnp.dot(pick, grad_ref[...], preferred_element_type=jnp.float32)
+        picked_grad = (picked_grad * spread).astype(jnp.bfloat16)
+        if k == 0:
+            grads[sec, block(0)] = picked_grad
+            for copy in s_copies(0):
+                copy.start()
+        else:
+            send_grads[k - 1] = picked_grad
+            z_copies(k)[1].start()
+
+    for load in loads:
+        load.wait()
+
+    def arrive(k):
+        for copy, onward in zip(z_copies(k), s_copies(k)):
+            copy.wait_recv()
+            onward.start()
+
+    def forward(k):
+        for copy in s_copies(k):
+            copy.wait_recv()
+        pre = jnp.dot(rows[0, block(k)], both_w[0:width, :], preferred_element_type=jnp.float32)
+        pre += jnp.dot(rows[1, block(k)], both_w[width : 2 * width, :], preferred_element_type=jnp.float32)
+        inner = contract_last(grads[0, block(k)], down_w[:, 0:width])
+        inner += contract_last(grads[1, block(k)], down_w[:, width : 2 * width])
+        for j in range(groups):
+            parts[k, j * slots : (j + 1) * slots, 0:256] = pre[:, j * 256 : (j + 1) * 256].astype(jnp.bfloat16)
+            parts[k, j * slots : (j + 1) * slots, 256:384] = inner[:, j * 128 : (j + 1) * 128].astype(jnp.bfloat16)
+        for r in far_first:
+            p_copy(k, r).start()
+
+    def reduce_local(k):
+        summed = parts[k, mine, :].astype(jnp.float32)
+        for r in range(1, n):
+            p_copy(k, r).wait_recv()
+            summed += got_parts[k, r - 1].astype(jnp.float32)
+        activated, gate_grad, up_grad = local_grads(summed[:, 0:128], summed[:, 128:256], summed[:, 256:384])
+        local[k, mine, 0:128] = gate_grad
+        local[k, mine, 128:256] = up_grad
+        local[k, mine, 256:384] = activated
+        for r in far_first:
+            a_copy(k, r).start()
+
+    def row_side(k, side):
+        span = pl.ds(pl.multiple_of(side * width, width), width)
+        return contract_last(gate_up(k), both_w[span, :])
+
+    def gate_up(k):
+        return jnp.concatenate(
+            [local[k, j * slots : (j + 1) * slots, 0:256] for j in range(groups)], axis=1
+        )
+
+    def active(k):
+        return jnp.concatenate(
+            [local[k, j * slots : (j + 1) * slots, 256:384] for j in range(groups)], axis=1
+        )
+
+    def backward(k):
+        for r in range(1, n):
+            a_copy(k, r).wait_recv()
+        halves[k] = row_side(k, other).astype(jnp.bfloat16)
+        h_copy(k).start()
+
+    def give_back(k):
+        own = row_side(k, sec)
+        h_copy(k).wait_recv()
+        whole = (own + got_half[k].astype(jnp.float32)).astype(jnp.bfloat16)
+        if k == 0:
+            returned[0] = whole
+        else:
+            back[k - 1] = whole
+            r_copy(k).start()
+
+    forward(0)
+    arrive(1)
+    reduce_local(0)
+    forward(1)
+    backward(0)
+    arrive(3)
+    reduce_local(1)
+    forward(3)
+    give_back(0)
+    backward(1)
+    arrive(2)
+    give_back(1)
+    forward(2)
+    reduce_local(3)
+    backward(3)
+    give_back(3)
+    reduce_local(2)
+    backward(2)
+    give_back(2)
+
+    chunk = 256
+    for side in range(2):
+        for low in range(0, width, chunk):
+            total = sum(
+                contract_rows(rows[side, block(k), low : low + chunk], gate_up(k)) for k in range(n)
+            ).astype(jnp.bfloat16)
+            start = side * width + low
+            for j in range(groups):
+                gate_g[start : start + chunk, j * 128 : (j + 1) * 128] = total[:, j * 256 : j * 256 + 128]
+                up_g[start : start + chunk, j * 128 : (j + 1) * 128] = total[:, j * 256 + 128 : (j + 1) * 256]
+    stores = [
+        pltpu.make_async_copy(gate_g, gate_out, io_sem.at[0]),
+        pltpu.make_async_copy(up_g, up_out, io_sem.at[1]),
+        pltpu.make_async_copy(down_g, down_out, io_sem.at[2]),
+    ]
+    stores[0].start()
+    stores[1].start()
+    for side in range(2):
+        for low in range(0, width, chunk):
+            start = side * width + low
+            down_g[:, start : start + chunk] = sum(
+                contract_rows(active(k), grads[side, block(k), low : low + chunk]) for k in range(n)
+            ).astype(jnp.bfloat16)
+    stores[2].start()
+
+    total = contract_rows(picks[0], returned[0])
+    for k in (1, 3, 2):
+        r_copy(k).wait_recv()
+        total += contract_rows(picks[k], returned[k])
+    token_out[...] = total.astype(jnp.bfloat16)
+
+    for k in range(n):
+        for copy in s_copies(k):
+            copy.wait_send()
+        h_copy(k).wait_send()
+        for r in range(1, n):
+            p_copy(k, r).wait_send()
+            a_copy(k, r).wait_send()
+        if k > 0:
+            for copy in z_copies(k):
+                copy.wait_send()
+            r_copy(k).wait_send()
+    for store in stores:
+        store.wait()
+
+
+def on_device_kernel(tokens, out_grad, expert_ids, combine, w_gate, w_up, w_down):
+    tok_dev, top_count = expert_ids.shape
+    n = lax.axis_size("expert")
+    capacity = (tok_dev * top_count * 9 + 8 * n - 1) // (8 * n)
+    slots = (capacity + 15) // 16 * 16
+    width = tokens.shape[1]
+    depth, hidden = w_gate.shape[1:]
+    groups = hidden // 128
+    share = (groups * slots + 16 * n - 1) // (16 * n) * 16
+    bf16 = jnp.bfloat16
+    vmem = pl.BlockSpec(memory_space=pltpu.VMEM)
+    hbm = pl.BlockSpec(memory_space=pl.ANY)
+    dma = pltpu.SemaphoreType.DMA
+    token_grad, gate_g, up_g, down_g = pl.pallas_call(
+        functools.partial(expert_kernel, n, slots),
+        out_shape=(
+            jax.ShapeDtypeStruct((tok_dev, width), bf16),
+            jax.ShapeDtypeStruct((depth, hidden), bf16),
+            jax.ShapeDtypeStruct((depth, hidden), bf16),
+            jax.ShapeDtypeStruct((hidden, depth), bf16),
+        ),
+        in_specs=[hbm, hbm, vmem, vmem, hbm, hbm, hbm],
+        out_specs=(vmem, hbm, hbm, hbm),
+        scratch_shapes=[
+            pltpu.VMEM((tok_dev, width), bf16),
+            pltpu.VMEM((tok_dev, width), bf16),
+            pltpu.VMEM((depth, 2 * hidden), bf16),
+            pltpu.VMEM((hidden, depth), bf16),
+            pltpu.VMEM((n, slots, tok_dev), bf16),
+            pltpu.VMEM((n - 1, slots, width), bf16),
+            pltpu.VMEM((n - 1, slots, width), bf16),
+            pltpu.VMEM((2, n * slots, width), bf16),
+            pltpu.VMEM((2, n * slots, width), bf16),
+            pltpu.VMEM((n, n * share, 384), bf16),
+            pltpu.VMEM((n, n - 1, share, 384), bf16),
+            pltpu.VMEM((n, n * share, 384), bf16),
+            pltpu.VMEM((n, slots, width), bf16),
+            pltpu.VMEM((n, slots, width), bf16),
+            pltpu.VMEM((n - 1, slots, width), bf16),
+            pltpu.VMEM((n, slots, width), bf16),
+            pltpu.VMEM((depth, hidden), bf16),
+            pltpu.VMEM((depth, hidden), bf16),
+            pltpu.VMEM((hidden, depth), bf16),
+            dma((3 + 2 * groups,)),
+            dma((2, n - 1)),
+            dma((2, n - 1)),
+            dma((2, n)),
+            dma((2, n)),
+            dma((n, n - 1)),
+            dma((n, n - 1)),
+            dma((n, n - 1)),
+            dma((n, n - 1)),
+            dma((n,)),
+            dma((n,)),
+            dma((n - 1,)),
+            dma((n - 1,)),
+        ],
+        compiler_params=pltpu.CompilerParams(
+            collective_id=0, has_side_effects=True, vmem_limit_bytes=48 * 1024 * 1024
+        ),
+    )(tokens, out_grad, expert_ids.T, combine.T, w_gate[0], w_up[0], w_down[0])
+    return (token_grad, gate_g[None], up_g[None], down_g[None])
+
+
+def fits_kernel(mesh):
+    shape = mesh.shape
+    return shape["section"] == 2 and shape["expert"] == 4 and shape["tp"] == 4
+
+
 def solution(mesh):
     return jax.shard_map(
-        on_device,
+        on_device_kernel if fits_kernel(mesh) else on_device,
         mesh=mesh,
         in_specs=(
             P("expert", ("tp", "section")),

time: 146 us -> 61.3 us (0.42)
  waiting for transfers between devices: 88.2 us -> 0 us
  Pallas kernels: 0 us -> 51.1 us
  matrix products: 14.8 us -> 0 us
  starting transfers between devices: 14.5 us -> 0 us
  between operations: 14.2 us -> 0.66 us
  blocking collectives: 4.53 us -> 0 us
  other arithmetic: 2.08 us -> 0 us
  local copies, waits for them, and re-layouts: 7.71 us -> 9.18 us
    pallas_call x0 -> x1, Pallas kernels: none -> 51.1 us  [on_device_kernel(): pl.pallas_call(functools.partial(expert_kernel, n, slots), out_shape=(jax...]
    psum x1 -> x0, waiting for transfers between devices: 46.9 us -> none  [on_device(): lax.psum(up_part.astype(jnp.bfloat16), 'tp').astype(jnp.float32)]
    all_to_all x3 -> x0, waiting for transfers between devices: 40 us -> none  [the longest x1 15.8 us: on_device(): lax.all_to_all(row_grad.reshape(experts, capacity, width_dev), 'expert',...]
    dot_general x11 -> x0, matrix products: 14.8 us -> none  [the longest x3 4.83 us: contract_rows(): lax.dot_general(left_side, right_side, (((0,), (0,)), ((), ())), preferre...]
    all_to_all x3 -> x0, starting transfers between devices: 14.4 us -> none  [the longest x1 6.21 us: on_device(): lax.all_to_all(send_rows, 'expert', split_axis=0, concat_axis=0, tiled=True)]
    unnamed x20 -> x18, local copies, waits for them, and re-layouts: 1.01 us -> 9.18 us
    all_gather x2 -> x0, blocking collectives: 4.53 us -> none  [the longest x1 2.41 us: on_device(): lax.all_gather(tokens, 'section', axis=1, tiled=True)]
    scatter x2 -> x0, local copies, waits for them, and re-layouts: 2.79 us -> none  [the longest x1 1.4 us: block_slots(): source = jnp.zeros((experts * capacity,), jnp.int32).at[place_index].set(...]
  transfers between devices with their start and end apart: 5 -> 0, of which waited for: 5 -> 0; matrix products, arithmetic and copies ran while one was open for 7% -> 0% of each run, Pallas kernels for 0% -> 0%
where the time goes in v2:
time: 61.3 us; the launch traced here: 61 us
  Pallas kernels  51.1 us (83%)
  local copies, waits for them, and re-layouts  9.18 us (15%)
  between operations  0.66 us (1%)
    pallas_call x1, Pallas kernels, on_device_kernel(): pl.pallas_call(functools.partial(expert_kernel, n, slots), out_shape=(jax...  51.1 us
    unnamed x18, local copies, waits for them, and re-layouts  9.18 us

profile of v2, /device:TPU:0, one launch (start us, length us, event | category | flops | bytes accessed | tf_op | source)
XLA Modules:
  0.0 61.0 jit_solution(12907553464329347983)
XLA Ops:
  0.6 0.0 copy-start.6
  0.6 0.0 copy-start.5
  0.7 0.7 %copy-done.6 = f32[128,2]{0,1:T(2,128)S(1)} copy-done((f32[128,2]{0,1:T(2,128)S(1)}, f32[128,2]{0,1:T(2,128)}, u32[]{:S(2)}) %copy-start.6) | copy-done | bytes 1048
  1.3 0.0 copy-done.5
  1.3 0.0 copy-start
  1.3 1.1 %copy-done = bf16[1,1024,384]{2,1,0:T(8,128)(2,1)S(1)} copy-done((bf16[1,1024,384]{2,1,0:T(8,128)(2,1)S(1)}, bf16[1,1024,384]{2,1,0:T(8,128)(2,1)}, u32[]{:S(2)}) %copy-start) | copy-done | bytes 786456
  2.5 0.0 copy-start.1
  2.5 1.1 %copy-done.1 = bf16[1,1024,384]{2,1,0:T(8,128)(2,1)S(1)} copy-done((bf16[1,1024,384]{2,1,0:T(8,128)(2,1)S(1)}, bf16[1,1024,384]{2,1,0:T(8,128)(2,1)}, u32[]{:S(2)}) %copy-start.1) | copy-done | bytes 786456
  3.6 0.0 copy-start.2
  3.6 1.1 %copy-done.2 = bf16[1,384,1024]{2,1,0:T(8,128)(2,1)S(1)} copy-done((bf16[1,384,1024]{2,1,0:T(8,128)(2,1)S(1)}, bf16[1,384,1024]{2,1,0:T(8,128)(2,1)}, u32[]{:S(2)}) %copy-start.2) | copy-done | bytes 786456
  4.7 0.0 copy-start.3
  4.7 0.9 %copy-done.3 = bf16[128,512]{1,0:T(8,128)(2,1)S(1)} copy-done((bf16[128,512]{1,0:T(8,128)(2,1)S(1)}, bf16[128,512]{1,0:T(8,128)(2,1)}, u32[]{:S(2)}) %copy-start.3) | copy-done | bytes 131096
  5.6 0.0 copy-start.4
  5.6 0.9 %copy-done.4 = bf16[128,512]{1,0:T(8,128)(2,1)S(1)} copy-done((bf16[128,512]{1,0:T(8,128)(2,1)S(1)}, bf16[128,512]{1,0:T(8,128)(2,1)}, u32[]{:S(2)}) %copy-start.4) | copy-done | bytes 131096
  6.5 51.1 %shard_map.102 = (bf16[128,512]{1,0:T(8,128)(2,1)S(1)}, bf16[1024,384]{1,0:T(8,128)(2,1)S(1)}, bf16[1024,384]{1,0:T(8,128)(2,1)S(1)}, bf16[384,1024]{1,0:T(8,128)(2,1)S(1)}) custom-call(bf16[128,512]{1,0:T(8,128)(2,1)S(1)} %copy-done.3, bf16[128,512]{1,0:T(8,128)(2,1)S(1)} %copy-done.4, s32[2,128]{1,0:T(2,128)S(1)} %bitcast.14, f32[2,128]{1,0:T(2,128)S(1)} %bitcast.15, ...), custom_call_target="tpu_custom_call" | custom-call | tf_op jit(solution)/shard_map/pallas_call | solution.py:458
  57.7 0.7 %copy.15 = bf16[128,512]{1,0:T(8,128)(2,1)} copy(bf16[128,512]{1,0:T(8,128)(2,1)S(1)} %get-tuple-element.16) | data formatting | bytes 262144
  58.3 0.9 %copy.16 = bf16[1,1024,384]{2,1,0:T(8,128)(2,1)} copy(bf16[1,1024,384]{2,1,0:T(8,128)(2,1)S(1)} %bitcast.10) | data formatting | bytes 1572864
  59.2 0.9 %copy.17 = bf16[1,1024,384]{2,1,0:T(8,128)(2,1)} copy(bf16[1,1024,384]{2,1,0:T(8,128)(2,1)S(1)} %bitcast.9) | data formatting | bytes 1572864
  60.1 0.9 %copy.18 = bf16[1,384,1024]{2,1,0:T(8,128)(2,1)} copy(bf16[1,384,1024]{2,1,0:T(8,128)(2,1)S(1)} %bitcast.8) | data formatting | bytes 1572864
Async XLA Ops:
  0.6 0.7 %copy-start.6 = (f32[128,2]{0,1:T(2,128)S(1)}, f32[128,2]{0,1:T(2,128)}, u32[]{:S(2)}) copy-start(f32[128,2]{0,1:T(2,128)} %param.10) | copy-start | bytes 3076
  0.6 0.7 %copy-start.5 = (s32[128,2]{0,1:T(2,128)S(1)}, s32[128,2]{0,1:T(2,128)}, u32[]{:S(2)}) copy-start(s32[128,2]{0,1:T(2,128)} %param.9) | copy-start | bytes 3076
  1.3 1.1 %copy-start = (bf16[1,1024,384]{2,1,0:T(8,128)(2,1)S(1)}, bf16[1,1024,384]{2,1,0:T(8,128)(2,1)}, u32[]{:S(2)}) copy-start(bf16[1,1024,384]{2,1,0:T(8,128)(2,1)} %param.11) | copy-start | bytes 2359300
  2.5 1.1 %copy-start.1 = (bf16[1,1024,384]{2,1,0:T(8,128)(2,1)S(1)}, bf16[1,1024,384]{2,1,0:T(8,128)(2,1)}, u32[]{:S(2)}) copy-start(bf16[1,1024,384]{2,1,0:T(8,128)(2,1)} %param.12) | copy-start | bytes 2359300
  3.6 1.1 %copy-start.2 = (bf16[1,384,1024]{2,1,0:T(8,128)(2,1)S(1)}, bf16[1,384,1024]{2,1,0:T(8,128)(2,1)}, u32[]{:S(2)}) copy-start(bf16[1,384,1024]{2,1,0:T(8,128)(2,1)} %param.13) | copy-start | bytes 2359300
  4.7 0.9 %copy-start.3 = (bf16[128,512]{1,0:T(8,128)(2,1)S(1)}, bf16[128,512]{1,0:T(8,128)(2,1)}, u32[]{:S(2)}) copy-start(bf16[128,512]{1,0:T(8,128)(2,1)} %tok_hbm.1) | copy-start | bytes 393220
  5.6 0.9 %copy-start.4 = (bf16[128,512]{1,0:T(8,128)(2,1)S(1)}, bf16[128,512]{1,0:T(8,128)(2,1)}, u32[]{:S(2)}) copy-start(bf16[128,512]{1,0:T(8,128)(2,1)} %grad_hbm.1) | copy-start | bytes 393220

commit v3 on v2

--- a/solution.py
+++ b/solution.py
@@ -150,6 +150,10 @@
     grad_ref,
     both_w,
     down_w,
+    both_t,
+    down_t,
+    both_acc,
+    down_acc,
     picks,
     send_rows,
     send_grads,
@@ -315,6 +319,9 @@
 
     for load in loads:
         load.wait()
+    for low in range(0, 2 * width, 256):
+        both_t[:, low : low + 256] = both_w[low : low + 256, :].T
+        down_t[low : low + 256, :] = down_w[:, low : low + 256].T
 
     def arrive(k):
         for copy, onward in zip(z_copies(k), s_copies(k)):
@@ -326,8 +333,8 @@
             copy.wait_recv()
         pre = jnp.dot(rows[0, block(k)], both_w[0:width, :], preferred_element_type=jnp.float32)
         pre += jnp.dot(rows[1, block(k)], both_w[width : 2 * width, :], preferred_element_type=jnp.float32)
-        inner = contract_last(grads[0, block(k)], down_w[:, 0:width])
-        inner += contract_last(grads[1, block(k)], down_w[:, width : 2 * width])
+        inner = jnp.dot(grads[0, block(k)], down_t[0:width, :], preferred_element_type=jnp.float32)
+        inner += jnp.dot(grads[1, block(k)], down_t[width : 2 * width, :], preferred_element_type=jnp.float32)
         for j in range(groups):
             parts[k, j * slots : (j + 1) * slots, 0:256] = pre[:, j * 256 : (j + 1) * 256].astype(jnp.bfloat16)
             parts[k, j * slots : (j + 1) * slots, 256:384] = inner[:, j * 128 : (j + 1) * 128].astype(jnp.bfloat16)
@@ -348,7 +355,7 @@
 
     def row_side(k, side):
         span = pl.ds(pl.multiple_of(side * width, width), width)
-        return contract_last(gate_up(k), both_w[span, :])
+        return jnp.dot(gate_up(k), both_t[:, span], preferred_element_type=jnp.float32)
 
     def gate_up(k):
         return jnp.concatenate(
@@ -375,6 +382,15 @@
         else:
             back[k - 1] = whole
             r_copy(k).start()
+
+    chunk = 256
+    pieces = [(side, low) for side in range(2) for low in range(0, width, chunk)]
+
+    def both_piece(side, low, blocks):
+        return sum(contract_rows(rows[side, block(k), low : low + chunk], gate_up(k)) for k in blocks)
+
+    def down_piece(side, low, blocks):
+        return sum(contract_rows(active(k), grads[side, block(k), low : low + chunk]) for k in blocks)
 
     forward(0)
     arrive(1)
@@ -392,20 +408,22 @@
     reduce_local(3)
     backward(3)
     give_back(3)
+    early = (0, 1, 3)
+    for side, low in pieces:
+        start = side * width + low
+        both_acc[start : start + chunk, :] = both_piece(side, low, early)
     reduce_local(2)
+    for side, low in pieces:
+        start = side * width + low
+        down_acc[:, start : start + chunk] = down_piece(side, low, early)
     backward(2)
     give_back(2)
-
-    chunk = 256
-    for side in range(2):
-        for low in range(0, width, chunk):
-            total = sum(
-                contract_rows(rows[side, block(k), low : low + chunk], gate_up(k)) for k in range(n)
-            ).astype(jnp.bfloat16)
-            start = side * width + low
-            for j in range(groups):
-                gate_g[start : start + chunk, j * 128 : (j + 1) * 128] = total[:, j * 256 : j * 256 + 128]
-                up_g[start : start + chunk, j * 128 : (j + 1) * 128] = total[:, j * 256 + 128 : (j + 1) * 256]
+    for side, low in pieces:
+        start = side * width + low
+        total = (both_acc[start : start + chunk, :] + both_piece(side, low, (2,))).astype(jnp.bfloat16)
+        for j in range(groups):
+            gate_g[start : start + chunk, j * 128 : (j + 1) * 128] = total[:, j * 256 : j * 256 + 128]
+            up_g[start : start + chunk, j * 128 : (j + 1) * 128] = total[:, j * 256 + 128 : (j + 1) * 256]
     stores = [
         pltpu.make_async_copy(gate_g, gate_out, io_sem.at[0]),
         pltpu.make_async_copy(up_g, up_out, io_sem.at[1]),
@@ -413,12 +431,11 @@
     ]
     stores[0].start()
     stores[1].start()
-    for side in range(2):
-        for low in range(0, width, chunk):
-            start = side * width + low
-            down_g[:, start : start + chunk] = sum(
-                contract_rows(active(k), grads[side, block(k), low : low + chunk]) for k in range(n)
-            ).astype(jnp.bfloat16)
+    for side, low in pieces:
+        start = side * width + low
+        down_g[:, start : start + chunk] = (
+            down_acc[:, start : start + chunk] + down_piece(side, low, (2,))
+        ).astype(jnp.bfloat16)
     stores[2].start()
 
     total = contract_rows(picks[0], returned[0])
@@ -442,6 +459,17 @@
         store.wait()
 
 
+def hand_over(*refs):
+    count = (len(refs) - 1) // 2
+    copies = [
+        pltpu.make_async_copy(refs[index], refs[count + index], refs[-1].at[index]) for index in range(count)
+    ]
+    for copy in copies:
+        copy.start()
+    for copy in copies:
+        copy.wait()
+
+
 def on_device_kernel(tokens, out_grad, expert_ids, combine, w_gate, w_up, w_down):
     tok_dev, top_count = expert_ids.shape
     n = lax.axis_size("expert")
@@ -455,7 +483,7 @@
     vmem = pl.BlockSpec(memory_space=pltpu.VMEM)
     hbm = pl.BlockSpec(memory_space=pl.ANY)
     dma = pltpu.SemaphoreType.DMA
-    token_grad, gate_g, up_g, down_g = pl.pallas_call(
+    results = pl.pallas_call(
         functools.partial(expert_kernel, n, slots),
         out_shape=(
             jax.ShapeDtypeStruct((tok_dev, width), bf16),
@@ -470,6 +498,10 @@
             pltpu.VMEM((tok_dev, width), bf16),
             pltpu.VMEM((depth, 2 * hidden), bf16),
             pltpu.VMEM((hidden, depth), bf16),
+            pltpu.VMEM((2 * hidden, depth), bf16),
+            pltpu.VMEM((depth, hidden), bf16),
+            pltpu.VMEM((depth, 2 * hidden), jnp.float32),
+            pltpu.VMEM((hidden, depth), jnp.float32),
             pltpu.VMEM((n, slots, tok_dev), bf16),
             pltpu.VMEM((n - 1, slots, width), bf16),
             pltpu.VMEM((n - 1, slots, width), bf16),
@@ -500,9 +532,17 @@
             dma((n - 1,)),
         ],
         compiler_params=pltpu.CompilerParams(
-            collective_id=0, has_side_effects=True, vmem_limit_bytes=48 * 1024 * 1024
+            collective_id=0, has_side_effects=True, vmem_limit_bytes=63 * 1024 * 1024
         ),
     )(tokens, out_grad, expert_ids.T, combine.T, w_gate[0], w_up[0], w_down[0])
+    token_grad, gate_g, up_g, down_g = pl.pallas_call(
+        hand_over,
+        out_shape=tuple(jax.ShapeDtypeStruct(result.shape, result.dtype) for result in results),
+        in_specs=[hbm] * 4,
+        out_specs=(hbm,) * 4,
+        scratch_shapes=[dma((4,))],
+        compiler_params=pltpu.CompilerParams(vmem_limit_bytes=63 * 1024 * 1024),
+    )(*results)
     return (token_grad, gate_g[None], up_g[None], down_g[None])
 
 

time: 61.3 us -> 130 us (2.12)
  Pallas kernels: 51.1 us -> 129 us
  local copies, waits for them, and re-layouts: 9.18 us -> 0 us
    pallas_call x0 -> x1, Pallas kernels: none -> 76.6 us  [on_device_kernel(): pl.pallas_call(hand_over, out_shape=tuple((jax.ShapeDtypeStruct(result.sh...]
    unnamed x18 -> x0, local copies, waits for them, and re-layouts: 9.18 us -> none
    pallas_call x1, Pallas kernels: 51.1 us -> 52.9 us  [on_device_kernel(): pl.pallas_call(functools.partial(expert_kernel, n, slots), out_shape=(jax...]
where the time goes in v3:
time: 130 us
  Pallas kernels  129 us (99%)
    pallas_call x1, Pallas kernels, on_device_kernel(): pl.pallas_call(hand_over, out_shape=tuple((jax.ShapeDtypeStruct(result.sh...  76.6 us
    pallas_call x1, Pallas kernels, on_device_kernel(): pl.pallas_call(functools.partial(expert_kernel, n, slots), out_shape=(jax...  52.9 us

profile of v3, /device:TPU:0, one launch (start us, length us, event | category | flops | bytes accessed | tf_op | source)
XLA Modules:
  0.0 130.1 jit_solution(11874126503743571228)
XLA Ops:
  0.6 52.9 %shard_map.102 = (bf16[128,512]{1,0:T(8,128)(2,1)}, bf16[1024,384]{1,0:T(8,128)(2,1)}, bf16[1024,384]{1,0:T(8,128)(2,1)}, bf16[384,1024]{1,0:T(8,128)(2,1)}) custom-call(bf16[128,512]{1,0:T(8,128)(2,1)} %tok_hbm.1, bf16[128,512]{1,0:T(8,128)(2,1)} %grad_hbm.1, s32[2,128]{1,0:T(2,128)} %bitcast.11, f32[2,128]{1,0:T(2,128)} %bitcast.12, ...), custom_call_target="tpu_custom_call" | custom-call | tf_op jit(solution)/shard_map/pallas_call | solution.py:486
  53.5 76.6 %shard_map.103 = (bf16[128,512]{1,0:T(8,128)(2,1)}, bf16[1024,384]{1,0:T(8,128)(2,1)}, bf16[1024,384]{1,0:T(8,128)(2,1)}, bf16[384,1024]{1,0:T(8,128)(2,1)}) custom-call(bf16[128,512]{1,0:T(8,128)(2,1)} %get-tuple-element.12.refs_0_, bf16[1024,384]{1,0:T(8,128)(2,1)} %get-tuple-element.13.refs_1_, bf16[1024,384]{1,0:T(8,128)(2,1)} %get-tuple-element.14.refs_2_, ...), custom_call_target="tpu_custom_call" | custom-call | tf_op jit(solution)/shard_map/pallas_call | solution.py:538

commit v4 on v2

--- a/solution.py
+++ b/solution.py
@@ -150,6 +150,10 @@
     grad_ref,
     both_w,
     down_w,
+    both_t,
+    down_t,
+    place_ref,
+    weight_ref,
     picks,
     send_rows,
     send_grads,
@@ -250,7 +254,7 @@
             parts[k, groups * slots :, :] = jnp.zeros((spare, 384), jnp.bfloat16)
 
     def block(k):
-        return pl.ds(k * slots, slots)
+        return pl.ds(pl.multiple_of(k * slots, 16), slots)
 
     def z_copies(k):
         goal = hop("expert", partner(k))
@@ -290,31 +294,44 @@
 
     for copy in fetch:
         copy.wait()
-    for turn, k in enumerate((1, 2, 0, 3)):
-        pick = (place[k : k + 1, :] == numbers).astype(jnp.float32)
-        spread = jnp.sum(pick * weight[k : k + 1, :], axis=1, keepdims=True)
+    place_ref[...] = place
+    weight_ref[...] = weight
+    pl.semaphore_wait(barrier, 2 * n - 1)
+
+    @pl.loop(1, n + 1)
+    def _(turn):
+        k = lax.rem(turn, n)
+        pick = (place_ref[pl.ds(k, 1), :] == numbers).astype(jnp.float32)
+        spread = jnp.sum(pick * weight_ref[pl.ds(k, 1), :], axis=1, keepdims=True)
         pick = pick.astype(jnp.bfloat16)
         picks[k] = pick
         picked = jnp.dot(pick, tok_ref[...], preferred_element_type=jnp.float32).astype(jnp.bfloat16)
-        if k == 0:
-            rows[sec, block(0)] = picked
-        else:
-            send_rows[k - 1] = picked
-            if turn == 0:
-                pl.semaphore_wait(barrier, 2 * n - 1)
-            z_copies(k)[0].start()
         picked_grad = jnp.dot(pick, grad_ref[...], preferred_element_type=jnp.float32)
         picked_grad = (picked_grad * spread).astype(jnp.bfloat16)
-        if k == 0:
+
+        @pl.when(k == 0)
+        def _():
+            rows[sec, block(0)] = picked
             grads[sec, block(0)] = picked_grad
             for copy in s_copies(0):
                 copy.start()
-        else:
+
+        @pl.when(k != 0)
+        def _():
+            send_rows[k - 1] = picked
             send_grads[k - 1] = picked_grad
-            z_copies(k)[1].start()
+            for copy in z_copies(k):
+                copy.start()
 
     for load in loads:
         load.wait()
+
+    @pl.loop(0, 2 * width // 256)
+    def _(index):
+        span = pl.ds(pl.multiple_of(index * 256, 256), 256)
+        both_t[:, span] = both_w[span, :].T
+        down_t[span, :] = down_w[:, span].T
+
 
     def arrive(k):
         for copy, onward in zip(z_copies(k), s_copies(k)):
@@ -326,8 +343,8 @@
             copy.wait_recv()
         pre = jnp.dot(rows[0, block(k)], both_w[0:width, :], preferred_element_type=jnp.float32)
         pre += jnp.dot(rows[1, block(k)], both_w[width : 2 * width, :], preferred_element_type=jnp.float32)
-        inner = contract_last(grads[0, block(k)], down_w[:, 0:width])
-        inner += contract_last(grads[1, block(k)], down_w[:, width : 2 * width])
+        inner = jnp.dot(grads[0, block(k)], down_t[0:width, :], preferred_element_type=jnp.float32)
+        inner += jnp.dot(grads[1, block(k)], down_t[width : 2 * width, :], preferred_element_type=jnp.float32)
         for j in range(groups):
             parts[k, j * slots : (j + 1) * slots, 0:256] = pre[:, j * 256 : (j + 1) * 256].astype(jnp.bfloat16)
             parts[k, j * slots : (j + 1) * slots, 256:384] = inner[:, j * 128 : (j + 1) * 128].astype(jnp.bfloat16)
@@ -348,7 +365,7 @@
 
     def row_side(k, side):
         span = pl.ds(pl.multiple_of(side * width, width), width)
-        return contract_last(gate_up(k), both_w[span, :])
+        return jnp.dot(gate_up(k), both_t[:, span], preferred_element_type=jnp.float32)
 
     def gate_up(k):
         return jnp.concatenate(
@@ -370,56 +387,67 @@
         own = row_side(k, sec)
         h_copy(k).wait_recv()
         whole = (own + got_half[k].astype(jnp.float32)).astype(jnp.bfloat16)
-        if k == 0:
+
+        @pl.when(k == 0)
+        def _():
             returned[0] = whole
-        else:
+
+        @pl.when(k != 0)
+        def _():
             back[k - 1] = whole
             r_copy(k).start()
 
-    forward(0)
-    arrive(1)
-    reduce_local(0)
-    forward(1)
-    backward(0)
-    arrive(3)
-    reduce_local(1)
-    forward(3)
-    give_back(0)
-    backward(1)
-    arrive(2)
-    give_back(1)
-    forward(2)
-    reduce_local(3)
-    backward(3)
-    give_back(3)
-    reduce_local(2)
-    backward(2)
-    give_back(2)
+
+    def nth(turn):
+        return jnp.where(turn < 2, turn, n + 1 - turn)
+
+    @pl.loop(0, n + 2)
+    def _(turn):
+        @pl.when(jnp.logical_and(turn > 0, turn < n))
+        def _():
+            arrive(nth(turn))
+
+        @pl.when(jnp.logical_and(turn > 0, turn <= n))
+        def _():
+            reduce_local(nth(turn - 1))
+
+        @pl.when(turn < n)
+        def _():
+            forward(nth(turn))
+
+        @pl.when(turn > 1)
+        def _():
+            give_back(nth(turn - 2))
+
+        @pl.when(jnp.logical_and(turn > 0, turn <= n))
+        def _():
+            backward(nth(turn - 1))
 
     chunk = 256
-    for side in range(2):
-        for low in range(0, width, chunk):
-            total = sum(
-                contract_rows(rows[side, block(k), low : low + chunk], gate_up(k)) for k in range(n)
-            ).astype(jnp.bfloat16)
-            start = side * width + low
-            for j in range(groups):
-                gate_g[start : start + chunk, j * 128 : (j + 1) * 128] = total[:, j * 256 : j * 256 + 128]
-                up_g[start : start + chunk, j * 128 : (j + 1) * 128] = total[:, j * 256 + 128 : (j + 1) * 256]
+
+    @pl.loop(0, 2 * width // chunk)
+    def _(piece):
+        per_side = width // chunk
+        side = piece // per_side
+        low = pl.ds(pl.multiple_of(lax.rem(piece, per_side) * chunk, chunk), chunk)
+        span = pl.ds(pl.multiple_of(piece * chunk, chunk), chunk)
+        total = sum(
+            contract_rows(rows[side, block(k), low], gate_up(k)) for k in range(n)
+        ).astype(jnp.bfloat16)
+        for j in range(groups):
+            gate_g[span, j * 128 : (j + 1) * 128] = total[:, j * 256 : j * 256 + 128]
+            up_g[span, j * 128 : (j + 1) * 128] = total[:, j * 256 + 128 : (j + 1) * 256]
+        down_g[:, span] = sum(
+            contract_rows(active(k), grads[side, block(k), low]) for k in range(n)
+        ).astype(jnp.bfloat16)
+
     stores = [
         pltpu.make_async_copy(gate_g, gate_out, io_sem.at[0]),
         pltpu.make_async_copy(up_g, up_out, io_sem.at[1]),
         pltpu.make_async_copy(down_g, down_out, io_sem.at[2]),
     ]
-    stores[0].start()
-    stores[1].start()
-    for side in range(2):
-        for low in range(0, width, chunk):
-            start = side * width + low
-            down_g[:, start : start + chunk] = sum(
-                contract_rows(active(k), grads[side, block(k), low : low + chunk]) for k in range(n)
-            ).astype(jnp.bfloat16)
-    stores[2].start()
+    for store in stores:
+        store.start()
 
     total = contract_rows(picks[0], returned[0])
     for k in (1, 3, 2):
@@ -442,6 +470,20 @@
         store.wait()
 
 
+def hand_over(count, *refs):
+    sources, results, held = refs[:count], refs[count : 2 * count], refs[2 * count : 3 * count]
+    load_sem, store_sem = refs[3 * count :]
+    loads = [pltpu.make_async_copy(sources[i], held[i], load_sem.at[i]) for i in range(count)]
+    stores = [pltpu.make_async_copy(held[i], results[i], store_sem.at[i]) for i in range(count)]
+    for load in loads:
+        load.start()
+    for load, store in zip(loads, stores):
+        load.wait()
+        store.start()
+    for store in stores:
+        store.wait()
+
+
 def on_device_kernel(tokens, out_grad, expert_ids, combine, w_gate, w_up, w_down):
     tok_dev, top_count = expert_ids.shape
     n = lax.axis_size("expert")
@@ -455,7 +497,7 @@
     vmem = pl.BlockSpec(memory_space=pltpu.VMEM)
     hbm = pl.BlockSpec(memory_space=pl.ANY)
     dma = pltpu.SemaphoreType.DMA
-    token_grad, gate_g, up_g, down_g = pl.pallas_call(
+    results = pl.pallas_call(
         functools.partial(expert_kernel, n, slots),
         out_shape=(
             jax.ShapeDtypeStruct((tok_dev, width), bf16),
@@ -470,6 +512,10 @@
             pltpu.VMEM((tok_dev, width), bf16),
             pltpu.VMEM((depth, 2 * hidden), bf16),
             pltpu.VMEM((hidden, depth), bf16),
+            pltpu.VMEM((2 * hidden, depth), bf16),
+            pltpu.VMEM((depth, hidden), bf16),
+            pltpu.VMEM((8, tok_dev), jnp.float32),
+            pltpu.VMEM((8, tok_dev), jnp.float32),
             pltpu.VMEM((n, slots, tok_dev), bf16),
             pltpu.VMEM((n - 1, slots, width), bf16),
             pltpu.VMEM((n - 1, slots, width), bf16),
@@ -500,9 +546,17 @@
             dma((n - 1,)),
         ],
         compiler_params=pltpu.CompilerParams(
-            collective_id=0, has_side_effects=True, vmem_limit_bytes=48 * 1024 * 1024
+            collective_id=0, has_side_effects=True, vmem_limit_bytes=63 * 1024 * 1024
         ),
     )(tokens, out_grad, expert_ids.T, combine.T, w_gate[0], w_up[0], w_down[0])
+    token_grad, gate_g, up_g, down_g = pl.pallas_call(
+        functools.partial(hand_over, 4),
+        out_shape=tuple(jax.ShapeDtypeStruct(result.shape, result.dtype) for result in results),
+        in_specs=[hbm] * 4,
+        out_specs=(hbm,) * 4,
+        scratch_shapes=[pltpu.VMEM(result.shape, bf16) for result in results] + [dma((4,)), dma((4,))],
+        compiler_params=pltpu.CompilerParams(vmem_limit_bytes=63 * 1024 * 1024),
+    )(*results)
     return (token_grad, gate_g[None], up_g[None], down_g[None])
 
 

time: 61.3 us -> 51.8 us (0.85)
  local copies, waits for them, and re-layouts: 9.18 us -> 0 us
    unnamed x18 -> x0, local copies, waits for them, and re-layouts: 9.18 us -> none
    pallas_call x1, Pallas kernels: 51.1 us -> 48.3 us  [on_device_kernel(): pl.pallas_call(functools.partial(expert_kernel, n, slots), out_shape=(jax...]
    pallas_call x0 -> x1, Pallas kernels: none -> 2.68 us  [on_device_kernel(): pl.pallas_call(functools.partial(hand_over, 4), out_shape=tuple((jax.Shap...]
where the time goes in v4:
time: 51.8 us; the launch traced here: 51.6 us
  Pallas kernels  50.9 us (98%)
  between operations  0.64 us (1%)
    pallas_call x1, Pallas kernels, on_device_kernel(): pl.pallas_call(functools.partial(expert_kernel, n, slots), out_shape=(jax...  48.3 us
    pallas_call x1, Pallas kernels, on_device_kernel(): pl.pallas_call(functools.partial(hand_over, 4), out_shape=tuple((jax.Shap...  2.68 us

profile of v4, /device:TPU:0, one launch (start us, length us, event | category | flops | bytes accessed | tf_op | source)
XLA Modules:
  0.0 51.6 jit_solution(11579764978564682281)
XLA Ops:
  0.6 48.3 %shard_map.102 = (bf16[128,512]{1,0:T(8,128)(2,1)}, bf16[1024,384]{1,0:T(8,128)(2,1)}, bf16[1024,384]{1,0:T(8,128)(2,1)}, bf16[384,1024]{1,0:T(8,128)(2,1)}) custom-call(bf16[128,512]{1,0:T(8,128)(2,1)} %tok_hbm.1, bf16[128,512]{1,0:T(8,128)(2,1)} %grad_hbm.1, s32[2,128]{1,0:T(2,128)} %bitcast.11, f32[2,128]{1,0:T(2,128)} %bitcast.12, ...), custom_call_target="tpu_custom_call" | custom-call | tf_op jit(solution)/shard_map/pallas_call | solution.py:500
  48.9 2.7 %shard_map.103 = (bf16[128,512]{1,0:T(8,128)(2,1)}, bf16[1024,384]{1,0:T(8,128)(2,1)}, bf16[1024,384]{1,0:T(8,128)(2,1)}, bf16[384,1024]{1,0:T(8,128)(2,1)}) custom-call(bf16[128,512]{1,0:T(8,128)(2,1)} %get-tuple-element.12.refs_0_, bf16[1024,384]{1,0:T(8,128)(2,1)} %get-tuple-element.13.refs_1_, bf16[1024,384]{1,0:T(8,128)(2,1)} %get-tuple-element.14.refs_2_, ...), custom_call_target="tpu_custom_call" | custom-call | tf_op jit(solution)/shard_map/pallas_call | solution.py:552

commit v5 on v4

--- a/solution.py
+++ b/solution.py
@@ -298,14 +298,23 @@
     weight_ref[...] = weight
     pl.semaphore_wait(barrier, 2 * n - 1)
 
-    @pl.loop(1, n + 1)
+    @pl.loop(0, n)
     def _(turn):
-        k = lax.rem(turn, n)
+        k = jnp.where(turn == 0, 1, jnp.where(turn == 1, 3, jnp.where(turn == 2, 0, 2)))
         pick = (place_ref[pl.ds(k, 1), :] == numbers).astype(jnp.float32)
         spread = jnp.sum(pick * weight_ref[pl.ds(k, 1), :], axis=1, keepdims=True)
         pick = pick.astype(jnp.bfloat16)
         picks[k] = pick
         picked = jnp.dot(pick, tok_ref[...], preferred_element_type=jnp.float32).astype(jnp.bfloat16)
+
+        @pl.when(k != 0)
+        def _():
+            send_rows[k - 1] = picked
+
+        @pl.when(jnp.logical_and(k != 0, k != 2))
+        def _():
+            z_copies(k)[0].start()
+
         picked_grad = jnp.dot(pick, grad_ref[...], preferred_element_type=jnp.float32)
         picked_grad = (picked_grad * spread).astype(jnp.bfloat16)
 
@@ -318,10 +327,11 @@
 
         @pl.when(k != 0)
         def _():
-            send_rows[k - 1] = picked
             send_grads[k - 1] = picked_grad
-            for copy in z_copies(k):
-                copy.start()
+
+        @pl.when(jnp.logical_and(k != 0, k != 2))
+        def _():
+            z_copies(k)[1].start()
 
     for load in loads:
         load.wait()
@@ -403,17 +413,23 @@
 
     @pl.loop(0, n + 2)
     def _(turn):
+        @pl.when(turn == 1)
+        def _():
+            for sent, copy in zip(z_copies(1), z_copies(2)):
+                sent.wait_send()
+                copy.start()
+
         @pl.when(jnp.logical_and(turn > 0, turn < n))
         def _():
             arrive(nth(turn))
 
+        @pl.when(turn < n)
+        def _():
+            forward(nth(turn))
+
         @pl.when(jnp.logical_and(turn > 0, turn <= n))
         def _():
             reduce_local(nth(turn - 1))
-
-        @pl.when(turn < n)
-        def _():
-            forward(nth(turn))
 
         @pl.when(turn > 1)
         def _():
@@ -463,8 +479,9 @@
             p_copy(k, r).wait_send()
             a_copy(k, r).wait_send()
         if k > 0:
-            for copy in z_copies(k):
-                copy.wait_send()
+            if k > 1:
+                for copy in z_copies(k):
+                    copy.wait_send()
             r_copy(k).wait_send()
     for store in stores:
         store.wait()

time: 51.8 us -> 55.4 us (1.069)
  Pallas kernels: 50.9 us -> 54.6 us
    pallas_call x1, Pallas kernels: 48.3 us -> 51.9 us  [on_device_kernel(): pl.pallas_call(functools.partial(expert_kernel, n, slots), out_shape=(jax...]
where the time goes in v5:
time: 55.4 us; the launch traced here: 55.2 us
  Pallas kernels  54.6 us (99%)
  between operations  0.64 us (1%)
    pallas_call x1, Pallas kernels, on_device_kernel(): pl.pallas_call(functools.partial(expert_kernel, n, slots), out_shape=(jax...  51.9 us
    pallas_call x1, Pallas kernels, on_device_kernel(): pl.pallas_call(functools.partial(hand_over, 4), out_shape=tuple((jax.Shap...  2.68 us

profile of v5, /device:TPU:0, one launch (start us, length us, event | category | flops | bytes accessed | tf_op | source)
XLA Modules:
  0.0 55.2 jit_solution(16688286029519350956)
XLA Ops:
  0.6 51.9 %shard_map.102 = (bf16[128,512]{1,0:T(8,128)(2,1)}, bf16[1024,384]{1,0:T(8,128)(2,1)}, bf16[1024,384]{1,0:T(8,128)(2,1)}, bf16[384,1024]{1,0:T(8,128)(2,1)}) custom-call(bf16[128,512]{1,0:T(8,128)(2,1)} %tok_hbm.1, bf16[128,512]{1,0:T(8,128)(2,1)} %grad_hbm.1, s32[2,128]{1,0:T(2,128)} %bitcast.11, f32[2,128]{1,0:T(2,128)} %bitcast.12, ...), custom_call_target="tpu_custom_call" | custom-call | tf_op jit(solution)/shard_map/pallas_call | solution.py:517
  52.6 2.7 %shard_map.103 = (bf16[128,512]{1,0:T(8,128)(2,1)}, bf16[1024,384]{1,0:T(8,128)(2,1)}, bf16[1024,384]{1,0:T(8,128)(2,1)}, bf16[384,1024]{1,0:T(8,128)(2,1)}) custom-call(bf16[128,512]{1,0:T(8,128)(2,1)} %get-tuple-element.12.refs_0_, bf16[1024,384]{1,0:T(8,128)(2,1)} %get-tuple-element.13.refs_1_, bf16[1024,384]{1,0:T(8,128)(2,1)} %get-tuple-element.14.refs_2_, ...), custom_call_target="tpu_custom_call" | custom-call | tf_op jit(solution)/shard_map/pallas_call | solution.py:569

commit v6 on v4

--- a/solution.py
+++ b/solution.py
@@ -329,7 +329,6 @@
     @pl.loop(0, 2 * width // 256)
     def _(index):
         span = pl.ds(pl.multiple_of(index * 256, 256), 256)
-        both_t[:, span] = both_w[span, :].T
         down_t[span, :] = down_w[:, span].T
 
 
@@ -415,6 +414,13 @@
         def _():
             forward(nth(turn))
 
+        @pl.when(turn == 0)
+        def _():
+            @pl.loop(0, 2 * width // 256)
+            def _(index):
+                span = pl.ds(pl.multiple_of(index * 256, 256), 256)
+                both_t[:, span] = both_w[span, :].T
+
         @pl.when(turn > 1)
         def _():
             give_back(nth(turn - 2))
@@ -431,14 +437,14 @@
         side = piece // per_side
         low = pl.ds(pl.multiple_of(lax.rem(piece, per_side) * chunk, chunk), chunk)
         span = pl.ds(pl.multiple_of(piece * chunk, chunk), chunk)
-        total = sum(
-            contract_rows(rows[side, block(k), low], gate_up(k)) for k in range(n)
+        total = contract_rows(
+            rows[side, :, low], jnp.concatenate([gate_up(k) for k in range(n)], axis=0)
         ).astype(jnp.bfloat16)
         for j in range(groups):
             gate_g[span, j * 128 : (j + 1) * 128] = total[:, j * 256 : j * 256 + 128]
             up_g[span, j * 128 : (j + 1) * 128] = total[:, j * 256 + 128 : (j + 1) * 256]
-        down_g[:, span] = sum(
-            contract_rows(active(k), grads[side, block(k), low]) for k in range(n)
+        down_g[:, span] = contract_rows(
+            jnp.concatenate([active(k) for k in range(n)], axis=0), grads[side, :, low]
         ).astype(jnp.bfloat16)
 
     stores = [

time: 51.8 us -> 51.8 us (level)
  no operation moved by 1% of the time
where the time goes in v6:
time: 51.8 us; the launch traced here: 51.6 us
  Pallas kernels  50.9 us (98%)
  between operations  0.64 us (1%)
    pallas_call x1, Pallas kernels, on_device_kernel(): pl.pallas_call(functools.partial(expert_kernel, n, slots), out_shape=(jax...  48.3 us
    pallas_call x1, Pallas kernels, on_device_kernel(): pl.pallas_call(functools.partial(hand_over, 4), out_shape=tuple((jax.Shap...  2.68 us

profile of v6, /device:TPU:0, one launch (start us, length us, event | category | flops | bytes accessed | tf_op | source)
XLA Modules:
  0.0 51.6 jit_solution(2261969929134948351)
XLA Ops:
  0.6 48.3 %shard_map.102 = (bf16[128,512]{1,0:T(8,128)(2,1)}, bf16[1024,384]{1,0:T(8,128)(2,1)}, bf16[1024,384]{1,0:T(8,128)(2,1)}, bf16[384,1024]{1,0:T(8,128)(2,1)}) custom-call(bf16[128,512]{1,0:T(8,128)(2,1)} %tok_hbm.1, bf16[128,512]{1,0:T(8,128)(2,1)} %grad_hbm.1, s32[2,128]{1,0:T(2,128)} %bitcast.11, f32[2,128]{1,0:T(2,128)} %bitcast.12, ...), custom_call_target="tpu_custom_call" | custom-call | tf_op jit(solution)/shard_map/pallas_call | solution.py:506
  48.9 2.7 %shard_map.103 = (bf16[128,512]{1,0:T(8,128)(2,1)}, bf16[1024,384]{1,0:T(8,128)(2,1)}, bf16[1024,384]{1,0:T(8,128)(2,1)}, bf16[384,1024]{1,0:T(8,128)(2,1)}) custom-call(bf16[128,512]{1,0:T(8,128)(2,1)} %get-tuple-element.12.refs_0_, bf16[1024,384]{1,0:T(8,128)(2,1)} %get-tuple-element.13.refs_1_, bf16[1024,384]{1,0:T(8,128)(2,1)} %get-tuple-element.14.refs_2_, ...), custom_call_target="tpu_custom_call" | custom-call | tf_op jit(solution)/shard_map/pallas_call | solution.py:558

commit v7 on v6

--- a/solution.py
+++ b/solution.py
@@ -406,10 +406,6 @@
         def _():
             arrive(nth(turn))
 
-        @pl.when(jnp.logical_and(turn > 0, turn <= n))
-        def _():
-            reduce_local(nth(turn - 1))
-
         @pl.when(turn < n)
         def _():
             forward(nth(turn))
@@ -420,6 +416,10 @@
             def _(index):
                 span = pl.ds(pl.multiple_of(index * 256, 256), 256)
                 both_t[:, span] = both_w[span, :].T
+
+        @pl.when(jnp.logical_and(turn > 0, turn <= n))
+        def _():
+            reduce_local(nth(turn - 1))
 
         @pl.when(turn > 1)
         def _():

time: 51.8 us -> 57.8 us (1.12)
  Pallas kernels: 50.9 us -> 57 us
    pallas_call x1, Pallas kernels: 48.3 us -> 54.3 us  [on_device_kernel(): pl.pallas_call(functools.partial(expert_kernel, n, slots), out_shape=(jax...]
where the time goes in v7:
time: 57.8 us; the launch traced here: 57.6 us
  Pallas kernels  57 us (99%)
  between operations  0.64 us (1%)
    pallas_call x1, Pallas kernels, on_device_kernel(): pl.pallas_call(functools.partial(expert_kernel, n, slots), out_shape=(jax...  54.3 us
    pallas_call x1, Pallas kernels, on_device_kernel(): pl.pallas_call(functools.partial(hand_over, 4), out_shape=tuple((jax.Shap...  2.68 us

profile of v7, /device:TPU:0, one launch (start us, length us, event | category | flops | bytes accessed | tf_op | source)
XLA Modules:
  0.0 57.6 jit_solution(10847727146514831126)
XLA Ops:
  0.6 54.3 %shard_map.102 = (bf16[128,512]{1,0:T(8,128)(2,1)}, bf16[1024,384]{1,0:T(8,128)(2,1)}, bf16[1024,384]{1,0:T(8,128)(2,1)}, bf16[384,1024]{1,0:T(8,128)(2,1)}) custom-call(bf16[128,512]{1,0:T(8,128)(2,1)} %tok_hbm.1, bf16[128,512]{1,0:T(8,128)(2,1)} %grad_hbm.1, s32[2,128]{1,0:T(2,128)} %bitcast.11, f32[2,128]{1,0:T(2,128)} %bitcast.12, ...), custom_call_target="tpu_custom_call" | custom-call | tf_op jit(solution)/shard_map/pallas_call | solution.py:506
  55.0 2.7 %shard_map.103 = (bf16[128,512]{1,0:T(8,128)(2,1)}, bf16[1024,384]{1,0:T(8,128)(2,1)}, bf16[1024,384]{1,0:T(8,128)(2,1)}, bf16[384,1024]{1,0:T(8,128)(2,1)}) custom-call(bf16[128,512]{1,0:T(8,128)(2,1)} %get-tuple-element.12.refs_0_, bf16[1024,384]{1,0:T(8,128)(2,1)} %get-tuple-element.13.refs_1_, bf16[1024,384]{1,0:T(8,128)(2,1)} %get-tuple-element.14.refs_2_, ...), custom_call_target="tpu_custom_call" | custom-call | tf_op jit(solution)/shard_map/pallas_call | solution.py:558
